TPU v7x, 32 devices: a whole 2x2x4 slice. The times are simulated.
32 devices in a mesh: row: 4 (over y, core), col: 8 (over z, x).
Axes of the slice: x: 2, y: 2, z: 4, core: 2. Of those that a mesh axis runs over, the one named last changes fastest.
Arguments:
- modes: float32 [48, 2, 32, 1024], P(None, None, 'row', 'col'), may hold values from -25 to 25
- mean_flow: float32 [2, 32, 1024], P(None, 'row', 'col'), may hold values from -5 to 5
- seeds: int32 [4096, 48], P(('row', 'col')), may hold values from 0 to 4095
- amplitudes: float32 [48], replicated, may hold values from 0.5 to 2
- water_mask: int32 [32, 1024], P('row', 'col'), may hold values 0 or 1
Outputs:
- new_modes: float32 [48, 2, 32, 1024], P(None, None, 'row', 'col')
- new_coeffs: float32 [4096, 48], P(('row', 'col'))
Inputs may be any that keep to these rules, and one draw needn't show every extreme that they name: `water_mask`: 1 marks a water cell, 0 a land cell.
All inputs are finite; a program needn't handle non-finite values. No bound on the sum of `water_mask` on one device may be relied on, other than what follows from the above.
Results may differ from a plain program's by a relative error of at most 0.0003.
Values sent between devices are 32-bit elements; how exact they have to be, the bound alone decides.
No kernel may reach another device: no remote copies, remote signals or barrier semaphores. Data moves between devices by JAX's collectives and lax.ppermute only.
A program may use at most 128 MiB of HBM per device.

v0:
```python
import functools
import math

import jax
import jax.numpy as jnp
import numpy as np
from jax import lax
from jax.experimental import pallas as pl
from jax.experimental.pallas import tpu as pltpu
from jax.sharding import PartitionSpec as P

TIME_STEP = 0.25
VISCOUS = 0.2
PRECISE = lax.Precision.HIGHEST
TILE = 8
LANES = 128
NT = (((1,), (1,)), ((), ()))
NN = (((1,), (0,)), ((), ()))


HALF_TILE = TILE // 2


def pair_start(block):
    return TILE * (TILE * block * (block - 1) // 2 + (HALF_TILE + 1) * block)


def pair_layout(count):
    blocks = count // TILE
    pairs = pair_start(blocks)
    padded = -(-(pairs + count + 2) // LANES) * LANES
    first = np.full((1, padded), -1, np.int32)
    second = np.full((1, padded), -1, np.int32)
    share = np.zeros((1, padded), np.float32)

    def put(row, j, k):
        first[0, row], second[0, row], share[0, row] = j, k, 0.5 if j == k else 1.0

    for block in range(blocks):
        row = pair_start(block)
        base = TILE * block
        for j in range(base):
            for r in range(TILE):
                put(row + TILE * j + r, j, base + r)
        row += TILE * base
        for n in range(HALF_TILE + 1):
            for r in range(TILE):
                if r >= n:
                    put(row + TILE * n + r, base + n, base + r)
                elif n < HALF_TILE:
                    put(row + TILE * n + r, base + TILE - n, base + TILE - n + r)
    share[0, pairs : pairs + count] = 1.0
    return pairs, padded, first, second, share


def pair_tiles(arrays, count):
    blocks = count // TILE
    ids = lax.broadcasted_iota(jnp.int32, (TILE, arrays[0].shape[1]), 0)

    def tile(block):
        return [a[TILE * block : TILE * block + TILE, :] for a in arrays]

    for j in range(count):
        leads = [a[j : j + 1, :] for a in arrays]
        for block in range(j // TILE + 1, blocks):
            yield pair_start(block) + TILE * j, leads, tile(block)
    for block in range(blocks):
        base = TILE * block
        for n in range(HALF_TILE + 1):
            leads, parts = [a[base + n : base + n + 1, :] for a in arrays], tile(block)
            if 0 < n < HALF_TILE:
                other = base + TILE - n
                leads = [jnp.where(ids < n, a[other : other + 1, :], lead) for a, lead in zip(arrays, leads)]
                parts = [jnp.where(ids < n, pltpu.roll(part, n, 0), part) for part in parts]
            yield pair_start(block) + TILE * (base + n), leads, parts


def flow_tiles(arrays, count):
    leads = [a[count : count + 1, :] for a in arrays]
    for block in range(count // TILE):
        rows = slice(TILE * block, TILE * block + TILE)
        yield pair_start(count // TILE) + TILE * block, leads, [a[rows, :] for a in arrays]


def dot32(left, right, dims):
    return lax.dot_general(left, right, dims, precision=PRECISE, preferred_element_type=jnp.float32)


def halves(values):
    high = values.astype(jnp.bfloat16)
    low = (values - high.astype(jnp.float32)).astype(jnp.bfloat16)
    return high, low


def stacked_halves(values):
    high, low = halves(values)
    return jnp.concatenate([high, low], axis=0)


def dot_halves(left_stack, right, dims):
    high, low = halves(right)
    both = lax.dot_general(left_stack, high, dims, preferred_element_type=jnp.float32)
    both += lax.dot_general(left_stack, low, dims, preferred_element_type=jnp.float32)
    rows = left_stack.shape[0] // 2
    return both[:rows] + both[rows:]


def lane_ids(rows):
    return lax.broadcasted_iota(jnp.int32, (rows, LANES), 1)


SECOND = 32
SIDE = 64


def put_lane(packed, ids, plane, lane, target):
    return jnp.where(ids == target, pltpu.roll(plane, (target - lane) % LANES, 1), packed)


def front_kernel(
    scale, modes, flow, water, seeds, strength, amplitudes, planes, col_first, col_last, sums, early, coeffs, rows
):
    step = coeffs.shape[0]
    total = modes.shape[0] // step
    nx = total // 2
    fields = planes.shape[1]
    planes[...] = jnp.zeros(planes.shape, jnp.float32)
    diagonal = lax.broadcasted_iota(jnp.int32, (step, step), 0) == lax.broadcasted_iota(jnp.int32, (step, step), 1)
    heights = jnp.sum(jnp.where(diagonal, amplitudes[...], 0.0), axis=1, keepdims=True)
    wave = jnp.cos(seeds[...].astype(jnp.float32) * (3.0 * math.pi / 8192.0))
    values = strength[...] * heights * (wave + (wave * wave - 0.5))
    coeffs[...] = values
    pairs = pair_start(step // TILE)
    fill_coeff_rows(values, rows)
    rows[pairs + step : pairs + step + 1, :] = jnp.ones((1, values.shape[1]), jnp.float32)
    moments = dot32(values, rows[...], NT)
    tiles = moments.shape[1] // LANES
    for tile in range(tiles):
        sums[tile * step : (tile + 1) * step, :] = moments[:, tile * LANES : (tile + 1) * LANES]
    ids = lane_ids(fields)
    first = jnp.zeros((fields, LANES), jnp.float32)
    last = jnp.zeros((fields, LANES), jnp.float32)
    gram = jnp.zeros((step, step), jnp.float32)
    for x in range(nx):
        mask = water[x : x + 1, :].astype(jnp.float32)
        both = []
        for c in range(2):
            q = 2 * x + c
            field = modes[pl.ds(c * nx + x, step, stride=total), :]
            both.append(field)
            planes[q + 4, 0:step, :] = field
            planes[q + 4, step : step + 1, :] = flow[c * nx + x : c * nx + x + 1, :]
            planes[q + 4, step + 1 : step + 2, :] = mask
            plane = planes[q + 4]
            first = put_lane(first, ids, plane, 0, q + 2)
            first = put_lane(first, ids, plane, 1, q + 2 + SECOND)
            last = put_lane(last, ids, plane, LANES - 1, q + 2)
            last = put_lane(last, ids, plane, LANES - 2, q + 2 + SECOND)
        wide = jnp.concatenate(both, axis=1)
        weight = jnp.concatenate([mask, mask], axis=1) * scale
        gram += dot_halves(stacked_halves(wide * weight), wide, NT)
    col_first[...] = first
    col_last[...] = last
    heads = lax.broadcasted_iota(jnp.int32, (step, step), 0)
    lanes = lax.broadcasted_iota(jnp.int32, (step, step), 1)
    both = jnp.where(lanes < heads, gram, moments[:, pairs : pairs + step])
    corner = jnp.sum(jnp.where(lanes == heads, gram, 0.0), axis=1, keepdims=True)
    rest = jnp.zeros((step, SIDE - step - 2), jnp.float32)
    packed = jnp.concatenate([both, moments[:, pairs + step : pairs + step + 1], corner, rest], axis=1)
    early[...] = jnp.concatenate([packed[: step // 2], packed[step // 2 :]], axis=1)


def fill_coeff_rows(values, rows):
    count = values.shape[0]
    pairs = pair_start(count // TILE)
    for start, (lead,), (part,) in pair_tiles([values], count):
        rows[start : start + TILE, :] = lead * part
    rows[pairs : pairs + count, :] = values
    rows[pairs + count :, :] = jnp.zeros((rows.shape[0] - pairs - count, values.shape[1]), jnp.float32)


def extend_kernel(planes, above, below, first_in, last_in, extended, col_first, col_last):
    total = planes.shape[0]
    fields = planes.shape[1]
    ids = lane_ids(fields)
    extended[0:4] = above[...]
    extended[4 : total - 4] = planes[4 : total - 4]
    extended[total - 4 :] = below[...]
    first = first_in[...]
    last = last_in[...]
    for c in range(2):
        for plane, lane in ((above[2 + c], c), (below[c], total - 6 + c)):
            first = put_lane(first, ids, plane, 0, lane)
            last = put_lane(last, ids, plane, LANES - 1, lane)
    col_first[...] = first
    col_last[...] = last


def plain_gradient_kernel(planes, grad_x, grad_y):
    fields = planes.shape[1]
    ids = lane_ids(fields)
    for q in range(grad_x.shape[0]):
        grad_x[q] = 0.5 * (planes[q + 6] - planes[q + 2])
        plane = planes[q + 4]
        east = jnp.where(ids == LANES - 1, 0.0, pltpu.roll(plane, LANES - 1, 1))
        west = jnp.where(ids == 0, 0.0, pltpu.roll(plane, 1, 1))
        grad_y[q] = 0.5 * (east - west)


def odd_even(packed, ids):
    odd = ids % 2 == 1
    zero = jnp.where(odd, pltpu.roll(packed, 1, 1), packed)
    one = jnp.where(odd, packed, pltpu.roll(packed, LANES - 1, 1))
    return zero, one


def gradient_kernel(extended, left, right, col_first, col_last, grad_x, grad_y, ring, shape):
    fields = extended.shape[1]
    ids = lane_ids(fields)
    from_left = left[...]
    from_right = right[...]
    for q in range(grad_x.shape[0]):
        grad_x[q] = 0.5 * (extended[q + 4] - extended[q])
        plane = extended[q + 2]
        east = put_lane(pltpu.roll(plane, LANES - 1, 1), ids, from_right, q, LANES - 1)
        west = put_lane(pltpu.roll(plane, 1, 1), ids, from_left, q, 0)
        grad_y[q] = 0.5 * (east - west)

    def both(near, far):
        return jnp.where(ids < SIDE, near, pltpu.roll(far, SIDE, 1))

    centre = both(from_left, from_right)
    inner = both(col_first[...], col_last[...])
    outer = pltpu.roll(centre, LANES - SECOND, 1)
    zero, one = odd_even(centre, ids)
    ring[0] = zero
    ring[1] = one
    ring[2] = 0.5 * (pltpu.roll(centre, LANES - 2, 1) - pltpu.roll(centre, 2, 1))
    ring[3] = jnp.where(ids < SIDE, 0.5, -0.5) * (inner - outer)
    ring[4] = centre

    total, count, _ = shape.shape
    beside = centre[0:count, :] * centre[count + 1 : count + 2, :]

    def masked(q):
        return extended[q + 2, 0:count, :] * extended[q + 2, count + 1 : count + 2, :]

    for q in range(total):
        water = extended[q + 4, count + 1 : count + 2, :]
        shape[q] = (TIME_STEP * water) * diffused(masked(q), masked(q + 2), masked(q + 4), beside, q)


def diffused(before, plane, after, beside, q):
    ids = lane_ids(plane.shape[0])
    east = put_lane(pltpu.roll(plane, LANES - 1, 1), ids, beside, q + 2 + SIDE, LANES - 1)
    west = put_lane(pltpu.roll(plane, 1, 1), ids, beside, q + 2, 0)
    return plane + VISCOUS * (before + after + east + west - 4.0 * plane)


def all_tiles(arrays):
    count = arrays[0].shape[0] // TILE * TILE - TILE
    yield from pair_tiles(arrays, count)
    yield from flow_tiles(arrays, count)


def fill_pair_fields(velocity, grads, rows):
    arrays = list(velocity) + [ref for pair in grads for ref in pair]
    for start, leads, parts in all_tiles(arrays):
        for c in range(len(grads)):
            x, y = 2 + 2 * c, 3 + 2 * c
            value = leads[0] * parts[x] + leads[1] * parts[y] + parts[0] * leads[x] + parts[1] * leads[y]
            rows[start : start + TILE, c * LANES : (c + 1) * LANES] = value


def fill_edge_fields(edges, rows):
    for start, leads, parts in all_tiles([ref for edge in edges for ref in edge]):
        for n in range(len(edges)):
            u, d = 2 * n, 2 * n + 1
            value = leads[u] * parts[d] + parts[u] * leads[d]
            rows[start : start + TILE, n * LANES : (n + 1) * LANES] = value


def clear_rest(rows, count):
    used = pair_start(count // TILE) + count
    rows[used:, :] = jnp.zeros((rows.shape[0] - used, rows.shape[1]), jnp.float32)


def add_to_tiles(out, before, stack, rows):
    count = stack.shape[0] // 2
    for first in range(0, rows.shape[0], 2 * LANES):
        last = min(first + 2 * LANES, rows.shape[0])
        value = dot_halves(stack, rows[first:last, :], NT)
        for start in range(first, last, LANES):
            place = slice(start // LANES * count, (start // LANES + 1) * count)
            part = value[:, start - first : start - first + LANES]
            out[place, :] = part if before is None else before[place, :] + part


def tiles_beside(values, count):
    return jnp.concatenate([values[at : at + count, :] for at in range(0, values.shape[0], count)], axis=1)


def tensor_kernel(scale, start, stop, planes, grad_x, grad_y, *refs):
    *before, out, rows = refs
    count = out.shape[0] * LANES // rows.shape[0]
    clear_rest(rows, count)
    out[...] = before[0][...] if before else jnp.zeros(out.shape, jnp.float32)

    def body(x, carry):
        q = 2 * x
        velocity = [planes.at[q + 4], planes.at[q + 5]]
        fill_pair_fields(velocity, [(grad_x.at[q + c], grad_y.at[q + c]) for c in range(2)], rows)
        water = planes[q + 4, count + 1 : count + 2, :] * (-scale)
        weighted = jnp.concatenate([planes[q + 4, 0:count, :] * water, planes[q + 5, 0:count, :] * water], axis=1)
        add_to_tiles(out, out, stacked_halves(weighted), rows)
        return carry

    lax.fori_loop(start, stop, body, 0)


def edge_tensor_kernel(scale, extended, left, right, col_first, col_last, before, out, parts, rows):
    count = out.shape[0] * LANES // rows.shape[0]
    total = extended.shape[0]
    fields = extended.shape[1]
    clear_rest(rows, count)
    ids = lane_ids(fields)
    for c in range(2):
        parts[c] = -0.5 * extended[2 + c]
        parts[2 + c] = 0.5 * extended[total - 4 + c]
    near = (ids >= 2) & (ids < total - 6)
    far = (ids >= 2 + SIDE) & (ids < total - 6 + SIDE)
    parts[4] = jnp.where(near, -0.5 * left[...], jnp.where(far, 0.5 * pltpu.roll(right[...], SIDE, 1), 0.0))
    centre = jnp.where(ids < SIDE, col_first[...], pltpu.roll(col_last[...], SIDE, 1))
    parts[5] = odd_even(centre, ids)[1]
    top, bottom = extended.at[4], extended.at[total - 6]
    fill_edge_fields(
        [
            (top, parts.at[0]), (top, parts.at[1]), (bottom, parts.at[2]), (bottom, parts.at[3]),
            (parts.at[5], parts.at[4]),
        ],
        rows,
    )
    weighted = []
    for plane in (extended[4], extended[5], extended[total - 6], extended[total - 5], centre):
        weighted.append(plane[0:count, :] * (plane[count + 1 : count + 2, :] * (-scale)))
    add_to_tiles(out, before, stacked_halves(jnp.concatenate(weighted, axis=1)), rows)


def inverse_pair(first, second):
    count = first.shape[0]
    row_ids = lax.broadcasted_iota(jnp.int32, (count, count), 0)
    col_ids = lax.broadcasted_iota(jnp.int32, (count, count), 1)
    both = [first, second]
    for k in range(count):
        for n in range(2):
            a = both[n]
            row = a[k : k + 1, :]
            col = a[:, k : k + 1]
            pivot = 1.0 / a[k : k + 1, k : k + 1]
            row = jnp.where(col_ids[0:1] == k, 1.0, row) * pivot
            kept = jnp.where(col_ids == k, 0.0, a)
            both[n] = jnp.where(row_ids == k, row, kept - col * row)
    return both


def inverse_kernel(realizations, early, first, second, share, cov_inverse, gram_inverse, mean, pair_cov, offset):
    count, padded = offset.shape
    packed = jnp.concatenate([early[:, 0:SIDE], early[:, SIDE : 2 * SIDE]], axis=0)
    shared = packed[:, 0:count]
    means = packed[:, count : count + 1] * (1.0 / realizations)
    row_ids = lax.broadcasted_iota(jnp.int32, (count, count), 0)
    col_ids = lax.broadcasted_iota(jnp.int32, (count, count), 1)
    turned = shared.T
    raw_second = jnp.where(col_ids >= row_ids, shared, turned) * (1.0 / realizations)
    gram = jnp.where(col_ids < row_ids, shared, turned)
    gram = jnp.where(col_ids == row_ids, packed[:, count + 1 : count + 2], gram)
    mean_row = jnp.sum(jnp.where(row_ids == col_ids, means, 0.0), axis=0, keepdims=True)
    covariance = raw_second - means * mean_row
    cov_inverse[...], gram_inverse[...] = inverse_pair(covariance, gram)
    ids = lax.broadcasted_iota(jnp.int32, (count, padded), 0)
    pick_first = (ids == first[...]).astype(jnp.float32)
    pick_second = (ids == second[...]).astype(jnp.float32)
    cov_first = dot32(covariance, pick_first, NN)
    cov_second = dot32(covariance, pick_second, NN)
    mean_first = jnp.sum(pick_first * means, axis=0, keepdims=True)
    mean_second = jnp.sum(pick_second * means, axis=0, keepdims=True)
    cov_pair = jnp.sum(pick_first * cov_second, axis=0, keepdims=True)
    offset[...] = means * (cov_pair + mean_first * mean_second) + mean_first * cov_second + mean_second * cov_first
    mean[...] = jnp.broadcast_to(means, mean.shape)
    pair_cov[...] = cov_pair * share[...]


def weight_kernel(realizations, sums, cov_inverse, offset, share, coeffs, mean, weights, pieces, rows):
    count = coeffs.shape[0]
    padded = weights.shape[1]
    pairs = pair_start(count // TILE)
    third = tiles_beside(sums[...], count) * (1.0 / realizations) - offset[...]
    weight_map = dot32(cov_inverse[...], third, NN) * share[...]
    ids = lax.broadcasted_iota(jnp.int32, (count, padded), 0)
    lanes = lax.broadcasted_iota(jnp.int32, (count, padded), 1)
    unit = jnp.where(lanes - pairs == ids, 1.0, 0.0)
    weights[...] = stacked_halves(jnp.where(lanes < pairs, weight_map, unit))
    fill_coeff_rows(coeffs[...] - mean[...], rows)
    pieces[...] = stacked_halves(rows[...])


def forcing_kernel(start, weights, extended, grad_x, grad_y, out, rows):
    count = weights.shape[0] // 2
    clear_rest(rows, count)
    stack = weights[...]

    def body(n, carry):
        q = 2 * (start + n)
        velocity = [extended.at[q + 2], extended.at[q + 3]]
        fill_pair_fields(velocity, [(grad_x.at[q + c], grad_y.at[q + c]) for c in range(2)], rows)
        nonlinear = dot_halves(stack, rows[...], NN)
        water = extended[q + 2, count + 1 : count + 2, :]
        for c in range(2):
            part = nonlinear[:, c * LANES : (c + 1) * LANES]
            out[2 * n + c] = water * (extended[q + 2 + c, 0:count, :] - TIME_STEP * part)
        return carry

    lax.fori_loop(0, out.shape[0] // 2, body, 0)


def ring_forcing_kernel(weights, ring, out, rows):
    count = weights.shape[0] // 2
    clear_rest(rows, count)
    fill_pair_fields([ring.at[0], ring.at[1]], [(ring.at[2], ring.at[3])], rows)
    nonlinear = dot_halves(weights[...], rows[...], NN)
    out[...] = ring[4, count + 1 : count + 2, :] * (ring[4, 0:count, :] - TIME_STEP * nonlinear)


def smooth_kernel(extended, moved, moved_ring, base):
    total, count, _ = base.shape
    beside = moved_ring[...]
    for q in range(total):
        water = extended[q + 4, count + 1 : count + 2, :]
        base[q] = water * diffused(moved[q], moved[q + 2], moved[q + 4], beside, q)


def finish_kernel(
    tensor, weights, pieces, gram_inverse, coeffs, mean, pair_cov, share, base, shape,
    modes_out, coeffs_out, new_modes, new_coeffs, sems,
):
    count = coeffs.shape[0]
    total = base.shape[0]
    inverse = gram_inverse[...]
    tens = tiles_beside(tensor[...], count)
    projected = dot_halves(weights[...], tens, NT)
    stack = stacked_halves(tens * share[...])
    drift = jnp.dot(stack, pieces[0 : tens.shape[1], :], preferred_element_type=jnp.float32)
    drift += jnp.dot(stack, pieces[tens.shape[1] :, :], preferred_element_type=jnp.float32)
    drift = drift[:count] + drift[count:] - jnp.sum(tens * pair_cov[...], axis=1, keepdims=True)
    solved = stacked_halves(dot32(projected, inverse, NN))
    new_coeffs[...] = coeffs[...] - mean[...] + TIME_STEP * dot32(inverse, drift, NN)
    for x in range(total // 2):
        both = jnp.concatenate([shape[2 * x], shape[2 * x + 1]], axis=1)
        change = dot_halves(solved, both, NN)
        for c in range(2):
            value = base[2 * x + c] - change[:, c * LANES : (c + 1) * LANES]
            new_modes[pl.ds(c * (total // 2) + x, count, stride=total), :] = value
    leaving = [
        pltpu.make_async_copy(new_coeffs, coeffs_out, sems.at[0]),
        pltpu.make_async_copy(new_modes, modes_out, sems.at[1]),
    ]
    for leave in leaving:
        leave.start()
    for leave in leaving:
        leave.wait()


def axis_bits(axis):
    count = lax.axis_size(axis)
    assert count & (count - 1) == 0
    return list(range(count.bit_length() - 1))


def swap(values, axis, partner):
    return lax.ppermute(values, axis, list(enumerate(partner)))


def pairs_a(axis):
    return [i ^ 1 for i in range(lax.axis_size(axis))]


def shifted(axis, distance):
    count = lax.axis_size(axis)
    return [(((i - 1) % count ^ distance) + 1) % count for i in range(count)]


def later_steps(axis):
    return [(axis, shifted(axis, 1 << bit)) for bit in axis_bits(axis)[2:]]


def with_edges(axis, partner, values, *edges):
    rows = [values.shape[0]] + [edge.shape[0] * edge.shape[1] for edge in edges]
    flat = [values] + [edge.reshape(-1, edge.shape[-1]) for edge in edges]
    arrived = swap(jnp.concatenate(flat, axis=0), axis, partner)
    ends = np.cumsum(rows)
    return [arrived[: rows[0]]] + [
        arrived[ends[n] : ends[n + 1]].reshape(edge.shape) for n, edge in enumerate(edges)
    ]


def neighbours(axis, from_a, from_b):
    here = lax.axis_index(axis)
    even = here % 2 == 0
    before = jnp.where(here == 0, 0.0, jnp.where(even, from_b, from_a))
    after = jnp.where(here == lax.axis_size(axis) - 1, 0.0, jnp.where(even, from_a, from_b))
    return before, after


def split(values, lower):
    half = values.shape[0] // 2
    top, bottom = values[:half], values[half:]
    return jnp.where(lower, top, bottom), jnp.where(lower, bottom, top)


def joined(kept, other, lower):
    return jnp.concatenate([jnp.where(lower, kept, other), jnp.where(lower, other, kept)], axis=0)


def tied(*values):
    return lax.optimization_barrier(values)


def shape32(*dims):
    return jax.ShapeDtypeStruct(dims, jnp.float32)


def vmem32(*dims):
    return pltpu.VMEM(dims, jnp.float32)


PARAMS = pltpu.CompilerParams(vmem_limit_bytes=32 * 1024 * 1024)


def on_device(modes, mean_flow, seeds, amplitudes, water_mask):
    count, _, nx, ny = modes.shape
    devices = lax.axis_size("row") * lax.axis_size("col")
    rows_dev = seeds.shape[0]
    row_total = rows_dev * devices
    scale = 1.0 / (2.0 * nx * ny * devices)
    pairs, padded, first, second, share = pair_layout(count)
    tiles = padded // LANES
    fields = count + TILE
    total = 2 * (nx + 4)
    assert ny == LANES and 2 * (nx + 2) <= SECOND and count % (2 * TILE) == 0
    call = functools.partial(pl.pallas_call, compiler_params=PARAMS)
    assert min(lax.axis_size("row"), lax.axis_size("col")) >= 4

    first_row = lax.axis_index(("row", "col")) * rows_dev
    row_ids = (first_row + jnp.arange(rows_dev, dtype=jnp.int32)).astype(jnp.float32)
    strength = (0.5 + row_ids / row_total).reshape(1, rows_dev)
    planes, own_first, own_last, sums, early, coeffs = call(
        functools.partial(front_kernel, scale),
        out_shape=(
            shape32(total, fields, ny), shape32(fields, ny), shape32(fields, ny),
            shape32(tiles * count, LANES), shape32(count // 2, LANES), shape32(count, rows_dev),
        ),
        scratch_shapes=[vmem32(padded, rows_dev)],
    )(
        modes.reshape(count * 2 * nx, ny), mean_flow.reshape(2 * nx, ny), water_mask, seeds.T,
        strength, amplitudes.reshape(1, count),
    )

    grads = call(
        plain_gradient_kernel, out_shape=(shape32(2 * nx, fields, ny), shape32(2 * nx, fields, ny))
    )(planes)

    def tensor_piece(number, grads, *before):
        start, stop = nx * number // 3, nx * (number + 1) // 3
        return call(
            functools.partial(tensor_kernel, scale, start, stop),
            out_shape=shape32(tiles * count, LANES),
            scratch_shapes=[vmem32(padded, 2 * ny)],
        )(planes, *grads, *before)

    top, bottom = planes[4:8], planes[total - 8 : total - 4]
    row, col = lax.axis_index("row"), lax.axis_index("col")
    even_row, even_col = row % 2 == 0, col % 2 == 0
    lower_a, lower_b = (row + 1) // 2 % 2 == 0, row % 2 == 1
    row_a, row_b = pairs_a("row"), shifted("row", 1)
    col_a, col_b = pairs_a("col"), shifted("col", 1)

    kept, sent = split(sums, lower_a)
    arrived, extra, row_from_a = with_edges("row", row_a, sent, early[None], jnp.where(even_row, bottom, top))
    kept, early, grads = tied(kept + arrived, early + extra[0], grads)
    kept, sent = split(kept, lower_b)
    arrived, extra, row_from_b = with_edges("row", row_b, sent, early[None], jnp.where(even_row, top, bottom))
    above, below = neighbours("row", row_from_a, row_from_b)
    tensor = tensor_piece(0, grads)
    kept, early, above, below, tensor = tied(kept + arrived, early + extra[0], above, below, tensor)
    extended, col_first, col_last = call(
        extend_kernel,
        out_shape=(shape32(total, fields, ny), shape32(fields, ny), shape32(fields, ny)),
    )(planes, above, below, own_first, own_last)
    first_edge, last_edge = col_first[None], col_last[None]
    arrived, extra, col_from_a = with_edges("col", col_a, kept, early[None], jnp.where(even_col, last_edge, first_edge))
    tensor = tensor_piece(1, grads, tensor)
    kept, early, tensor = tied(kept + arrived, early + extra[0], tensor)
    arrived, extra, col_from_b = with_edges("col", col_b, kept, early[None], jnp.where(even_col, first_edge, last_edge))
    left, right = (edge[0] for edge in neighbours("col", col_from_a, col_from_b))
    tensor = tensor_piece(2, grads, tensor)
    kept, early, left, right, tensor = tied(kept + arrived, early + extra[0], left, right, tensor)

    later = later_steps("row") + later_steps("col")
    for number, (axis, partner) in enumerate(later):
        arrived, extra = with_edges(axis, partner, kept, early[None])
        kept, early = kept + arrived, early + extra[0]
        if number == 0:
            tensor = call(
                functools.partial(edge_tensor_kernel, scale),
                out_shape=shape32(tiles * count, LANES),
                scratch_shapes=[vmem32(6, fields, ny), vmem32(padded, 5 * ny)],
            )(extended, left, right, col_first, col_last, tensor)
            grad_x, grad_y, ring, shape = call(
                gradient_kernel,
                out_shape=(
                    shape32(total - 4, fields, ny), shape32(total - 4, fields, ny), shape32(5, fields, ny),
                    shape32(2 * nx, count, ny),
                ),
            )(extended, left, right, col_first, col_last)
        kept, early, tensor, shape = tied(kept, early, tensor, shape)
    moments = kept

    kept, sent = split(tensor, lower_a)
    kept, moments = tied(kept + swap(sent, "row", row_a), moments)
    kept, sent = split(kept, lower_b)
    arrived, other = with_edges("row", row_b, sent, moments[None])
    kept = kept + arrived
    cov_inverse, gram_inverse, mean, pair_cov, offset = call(
        functools.partial(inverse_kernel, row_total),
        out_shape=(
            shape32(count, count), shape32(count, count), shape32(count, rows_dev), shape32(1, padded),
            shape32(count, padded),
        ),
    )(early, first, second, share)
    moments = joined(moments, other[0], lower_b)
    kept, moments, offset = tied(kept, moments, offset)
    sums = joined(moments, swap(moments, "row", row_a), lower_a)
    kept, sums = tied(kept, sums)
    weights, pieces = call(
        functools.partial(weight_kernel, row_total),
        out_shape=(
            jax.ShapeDtypeStruct((2 * count, padded), jnp.bfloat16),
            jax.ShapeDtypeStruct((2 * padded, rows_dev), jnp.bfloat16),
        ),
        scratch_shapes=[vmem32(padded, rows_dev)],
    )(sums, cov_inverse, offset, share, coeffs, mean)
    col_bits = axis_bits("col")
    steps = later_steps("row") + [
        ("col", [i ^ (1 << bit) for i in range(lax.axis_size("col"))]) for bit in col_bits[-1:] + col_bits[:-1]
    ]

    def forcing(start, stop):
        return call(
            functools.partial(forcing_kernel, start),
            out_shape=shape32(2 * (stop - start), count, ny),
            scratch_shapes=[vmem32(padded, 2 * ny)],
        )(weights, extended, grad_x, grad_y)

    def ring_forcing():
        return call(ring_forcing_kernel, out_shape=shape32(count, ny), scratch_shapes=[vmem32(padded, ny)])(
            weights, ring
        )

    ends = [(nx + 2) * n // 10 for n in (0, 4, 7, 10)]
    works = [functools.partial(forcing, ends[n], ends[n + 1]) for n in range(3)] + [ring_forcing]
    moved = []
    for axis, partner in steps:
        total_kept = kept + swap(kept, axis, partner)
        if works:
            moved.append(works.pop(0)())
        kept, weights, moved = tied(total_kept, weights, moved)
    kept = joined(kept, swap(kept, "row", row_b), lower_b)
    while works:
        moved.append(works.pop(0)())
    base = call(smooth_kernel, out_shape=shape32(2 * nx, count, ny))(
        extended, jnp.concatenate(moved[:-1], axis=0), moved[-1]
    )
    kept, base = tied(kept, base)
    tensor = joined(kept, swap(kept, "row", row_a), lower_a)

    new_modes, new_coeffs = call(
        finish_kernel,
        out_shape=(shape32(count * 2 * nx, ny), shape32(count, rows_dev)),
        out_specs=(pl.BlockSpec(memory_space=pltpu.HBM),) * 2,
        scratch_shapes=[vmem32(count * 2 * nx, ny), vmem32(count, rows_dev), pltpu.SemaphoreType.DMA((2,))],
    )(tensor, weights, pieces, gram_inverse, coeffs, mean, pair_cov, share, base, shape)
    return (new_modes.reshape(modes.shape), new_coeffs.T)


def solution(mesh):
    return jax.shard_map(
        on_device,
        mesh=mesh,
        in_specs=(
            P(None, None, "row", "col"),
            P(None, "row", "col"),
            P(("row", "col"), None),
            P(),
            P("row", "col"),
        ),
        out_specs=(P(None, None, "row", "col"), P(("row", "col"), None)),
        check_vma=False,
    )
```

profile of v0, /device:TPU:0, one launch (start us, length us, event | category | flops | bytes accessed | tf_op | source)
XLA Modules:
  0.0 62.5 jit_solution(11324411885635498530)
XLA Ops:
  0.7 0.0 copy-start.6
  0.7 0.7 %copy-done.2 = s32[128,48]{0,1:T(8,128)S(1)} copy-done((s32[128,48]{0,1:T(8,128)S(1)}, s32[128,48]{0,1:T(8,128)}, u32[]{:S(2)}) %copy-start.2) | copy-done | bytes 24600
  1.4 0.0 copy-done.6
  1.4 1.0 %copy-done = f32[48,2,8,128]{3,2,1,0:T(8,128)S(1)} copy-done((f32[48,2,8,128]{3,2,1,0:T(8,128)S(1)}, f32[48,2,8,128]{3,2,1,0:T(8,128)}, u32[]{:S(2)}) %copy-start) | copy-done | bytes 393240
  2.4 1.3 %shard_map.95 = (f32[24,56,128]{2,1,0:T(8,128)S(1)}, f32[56,128]{1,0:T(8,128)S(1)}, f32[56,128]{1,0:T(8,128)S(1)}, f32[480,128]{1,0:T(8,128)S(1)}, f32[24,128]{1,0:T(8,128)S(1)}, /*index=5*/f32[48,128]{1,0:T(8,128)S(1)}) custom-call(f32[768,128]{1,0:T(8,128)S(1)} %bitcast.12, f32[16,128]{1,0:T(8,128)S(1)} %bitcast.14, s32[8,128]{1,0:T(8,128)S(1)} %copy-done.6, ...), custom_call_target="tpu_custom_call" | custom-call | tf_op jit(solution)/shard_map/pallas_call | solution.py:556
  3.7 0.5 collective-permute-start
  4.3 0.3 shard_map.96
  4.6 0.8 %collective-permute-done = f32[488,128]{1,0:T(8,128)S(1)} collective-permute-done((f32[488,128]{1,0:T(8,128)S(1)}, f32[488,128]{1,0:T(8,128)S(1)}, u32[]{:S(2)}, u32[]{:S(2)}) %collective-permute-start) | collective-permute-done | bytes 249888 | tf_op jit(solution)/shard_map/ppermute | solution.py:480
  5.5 2.7 %collective-permute-start.1 = (f32[368,128]{1,0:T(8,128)S(1)}, f32[368,128]{1,0:T(8,128)S(1)}, u32[]{:S(2)}, u32[]{:S(2)}) collective-permute-start(f32[368,128]{1,0:T(8,128)S(1)} %pad_maximum_fusion.4), channel_id=1, source_target_pairs={{0,24},{8,16},{16,8},{24,0},{1,25},{9,17},{17,9},{25,1},{2,26},{10... | collective-permute-start | bytes 565256 | tf_op jit(solution)/shard_map/ppermute | solution.py:480
  8.2 1.5 %shard_map.97.refs_0_ = f32[480,128]{1,0:T(8,128)S(1)} custom-call(f32[24,56,128]{2,1,0:T(8,128)S(1)} %get-tuple-element.70.planes, f32[16,56,128]{2,1,0:T(8,128)S(1)} %get-tuple-element.75.grad_x, f32[16,56,128]{2,1,0:T(8,128)S(1)} %get-tuple-element.76.grad_y), custom_call_target="tpu_custom_call" | custom-call | tf_op jit(solution)/shard_map/pallas_call | solution.py:574
  9.7 3.3 %collective-permute-done.1 = f32[368,128]{1,0:T(8,128)S(1)} collective-permute-done((f32[368,128]{1,0:T(8,128)S(1)}, f32[368,128]{1,0:T(8,128)S(1)}, u32[]{:S(2)}, u32[]{:S(2)}) %collective-permute-start.1) | collective-permute-done | bytes 188448 | tf_op jit(solution)/shard_map/ppermute | solution.py:480
  13.0 0.1 shard_map.98
  13.2 2.2 %collective-permute-start.2 = (f32[200,128]{1,0:T(8,128)S(1)}, f32[200,128]{1,0:T(8,128)S(1)}, u32[]{:S(2)}, u32[]{:S(2)}) collective-permute-start(f32[200,128]{1,0:T(8,128)S(1)} %pad_maximum_fusion.8), channel_id=1, source_target_pairs={{0,1},{1,0},{2,3},{3,2},{4,5},{5,4},{6,7},{7,6},{8,9},{9,8},{10,11... | collective-permute-start | bytes 307208 | tf_op jit(solution)/shard_map/ppermute | solution.py:480
  15.4 2.2 %shard_map.99.refs_0_ = f32[480,128]{1,0:T(8,128)S(1)} custom-call(f32[24,56,128]{2,1,0:T(8,128)S(1)} %get-tuple-element.70.planes, f32[16,56,128]{2,1,0:T(8,128)S(1)} %get-tuple-element.75.grad_x, f32[16,56,128]{2,1,0:T(8,128)S(1)} %get-tuple-element.76.grad_y, f32[480,128]{1,0:T(8,128)S(1)} %shard_map.97.refs_0_), custom_call_target="tpu_custom_call" | custom-call | tf_op jit(solution)/shard_map/pallas_call | solution.py:574
  17.7 0.9 %collective-permute-done.2 = f32[200,128]{1,0:T(8,128)S(1)} collective-permute-done((f32[200,128]{1,0:T(8,128)S(1)}, f32[200,128]{1,0:T(8,128)S(1)}, u32[]{:S(2)}, u32[]{:S(2)}) %collective-permute-start.2) | collective-permute-done | bytes 102432 | tf_op jit(solution)/shard_map/ppermute | solution.py:480
  18.6 4.8 %collective-permute-start.3 = (f32[200,128]{1,0:T(8,128)S(1)}, f32[200,128]{1,0:T(8,128)S(1)}, u32[]{:S(2)}, u32[]{:S(2)}) collective-permute-start(f32[200,128]{1,0:T(8,128)S(1)} %pad_maximum_fusion.9), channel_id=1, source_target_pairs={{0,7},{1,2},{2,1},{3,4},{4,3},{5,6},{6,5},{7,0},{8,15},{9,10},{10,... | collective-permute-start | bytes 307208 | tf_op jit(solution)/shard_map/ppermute | solution.py:480
  23.5 2.3 %shard_map.100.before = f32[480,128]{1,0:T(8,128)S(1)} custom-call(f32[24,56,128]{2,1,0:T(8,128)S(1)} %get-tuple-element.70.planes, f32[16,56,128]{2,1,0:T(8,128)S(1)} %get-tuple-element.75.grad_x, f32[16,56,128]{2,1,0:T(8,128)S(1)} %get-tuple-element.76.grad_y, f32[480,128]{1,0:T(8,128)S(1)} %shard_map.99.refs_0_), custom_call_target="tpu_custom_call" | custom-call | tf_op jit(solution)/shard_map/pallas_call | solution.py:574
  25.7 0.4 collective-permute-done.3
  26.2 1.0 %collective-permute-start.4 = (f32[144,128]{1,0:T(8,128)S(1)}, f32[144,128]{1,0:T(8,128)S(1)}, u32[]{:S(2)}, u32[]{:S(2)}) collective-permute-start(f32[144,128]{1,0:T(8,128)S(1)} %pad_maximum_fusion.10), channel_id=1, source_target_pairs={{0,4},{1,5},{2,6},{3,7},{4,0},{5,1},{6,2},{7,3},{8,12},{9,13},{10,... | collective-permute-start | bytes 221192 | tf_op jit(solution)/shard_map/ppermute | solution.py:480
  27.2 1.2 %shard_map.102 = (f32[20,56,128]{2,1,0:T(8,128)S(1)}, f32[20,56,128]{2,1,0:T(8,128)S(1)}, f32[5,56,128]{2,1,0:T(8,128)S(1)}, f32[16,48,128]{2,1,0:T(8,128)S(1)}) custom-call(f32[24,56,128]{2,1,0:T(8,128)S(1)} %get-tuple-element.91.extended, f32[56,128]{1,0:T(8,128)S(1)} %get-tuple-element.92.left, f32[56,128]{1,0:T(8,128)S(1)} %get-tuple-element.93.right, ...), custom_call_target="tpu_custom_call" | custom-call | tf_op jit(solution)/shard_map/pallas_call | solution.py:618
  28.4 1.3 %shard_map.101 = f32[480,128]{1,0:T(8,128)S(1)} custom-call(f32[24,56,128]{2,1,0:T(8,128)S(1)} %get-tuple-element.91.extended, f32[56,128]{1,0:T(8,128)S(1)} %get-tuple-element.92.left, f32[56,128]{1,0:T(8,128)S(1)} %get-tuple-element.93.right, f32[56,128]{1,0:T(8,128)S(1)} %get-tuple-element.84.col_first, f32[56,128]{1,0:T(8,128)S(1)} %get-tuple-element.83.col_last, ...), custom_call_target="tpu_custom_call" | custom-call | tf_op jit(solution)/shard_map/pallas_call | solution.py:613
  29.7 2.0 %collective-permute-done.4 = f32[144,128]{1,0:T(8,128)S(1)} collective-permute-done((f32[144,128]{1,0:T(8,128)S(1)}, f32[144,128]{1,0:T(8,128)S(1)}, u32[]{:S(2)}, u32[]{:S(2)}) %collective-permute-start.4) | collective-permute-done | bytes 73760 | tf_op jit(solution)/shard_map/ppermute | solution.py:480
  31.7 0.1 collective-permute-start.5
  31.8 1.3 %collective-permute-done.5 = f32[240,128]{1,0:T(8,128)S(1)} collective-permute-done((f32[240,128]{1,0:T(8,128)S(1)}, f32[240,128]{1,0:T(8,128)S(1)}, u32[]{:S(2)}, u32[]{:S(2)}) %collective-permute-start.5) | collective-permute-done | bytes 122912 | tf_op jit(solution)/shard_map/ppermute | solution.py:480
  33.2 0.0 copy-start.1
  33.2 0.0 copy-start.4
  33.2 0.0 copy-start.5
  33.2 1.3 %collective-permute-start.6 = (f32[240,128]{1,0:T(8,128)S(1)}, f32[240,128]{1,0:T(8,128)S(1)}, u32[]{:S(2)}, u32[]{:S(2)}) collective-permute-start(f32[240,128]{1,0:T(8,128)S(1)} %pad_maximum_fusion.5), channel_id=1, source_target_pairs={{0,24},{8,16},{16,8},{24,0},{1,25},{9,17},{17,9},{25,1},{2,26},{10... | collective-permute-start | bytes 368648 | tf_op jit(solution)/shard_map/ppermute | solution.py:480
  34.6 4.3 %shard_map.103 = (f32[48,48]{1,0:T(8,128)S(1)}, f32[48,48]{1,0:T(8,128)S(1)}, f32[48,128]{1,0:T(8,128)S(1)}, f32[1,1280]{1,0:T(1,128)S(1)}, f32[48,1280]{1,0:T(8,128)S(1)}) custom-call(f32[24,128]{1,0:T(8,128)S(1)} %slice_add_fusion.6.early, s32[1,1280]{1,0:T(1,128)S(1)} %copy-done.5, s32[1,1280]{1,0:T(1,128)S(1)} %copy-done.4, f32[1,1280]{1,0:T(1,128)S(1)} %copy-done.1), custom_call_target="tpu_custom_call" | custom-call | tf_op jit(solution)/shard_map/pallas_call | solution.py:633
  38.9 0.4 collective-permute-start.7
  39.4 1.0 %collective-permute-done.7 = f32[240,128]{1,0:T(8,128)S(1)} collective-permute-done((f32[240,128]{1,0:T(8,128)S(1)}, f32[240,128]{1,0:T(8,128)S(1)}, u32[]{:S(2)}, u32[]{:S(2)}) %collective-permute-start.7) | collective-permute-done | bytes 122912 | tf_op jit(solution)/shard_map/ppermute | solution.py:480
  40.4 0.9 %collective-permute-start.8 = (f32[120,128]{1,0:T(8,128)S(1)}, f32[120,128]{1,0:T(8,128)S(1)}, u32[]{:S(2)}, u32[]{:S(2)}) collective-permute-start(f32[120,128]{1,0:T(8,128)S(1)} %get-tuple-element.104), channel_id=1, source_target_pairs={{0,4},{1,5},{2,6},{3,7},{4,0},{5,1},{6,2},{7,3},{8,12},{9,13},{10,... | collective-permute-start | bytes 184328 | tf_op jit(solution)/shard_map/ppermute | solution.py:480
  41.3 0.4 shard_map.104
  41.8 2.6 %shard_map.105 = f32[8,48,128]{2,1,0:T(8,128)S(1)} custom-call(bf16[96,1280]{1,0:T(8,128)(2,1)S(1)} %get-tuple-element.124.weights, f32[24,56,128]{2,1,0:T(8,128)S(1)} %get-tuple-element.91.extended, f32[20,56,128]{2,1,0:T(8,128)S(1)} %get-tuple-element.111.grad_x, f32[20,56,128]{2,1,0:T(8,128)S(1)} %get-tuple-element.112.grad_y), custom_call_target="tpu_custom_call" | custom-call | tf_op jit(solution)/shard_map/pallas_call | solution.py:658
  44.3 2.4 %collective-permute-done.8 = f32[120,128]{1,0:T(8,128)S(1)} collective-permute-done((f32[120,128]{1,0:T(8,128)S(1)}, f32[120,128]{1,0:T(8,128)S(1)}, u32[]{:S(2)}, u32[]{:S(2)}) %collective-permute-start.8) | collective-permute-done | bytes 61472 | tf_op jit(solution)/shard_map/ppermute | solution.py:480
  46.8 0.1 collective-permute-start.9
  46.9 1.9 %shard_map.106 = f32[6,48,128]{2,1,0:T(8,128)S(1)} custom-call(bf16[96,1280]{1,0:T(8,128)(2,1)S(1)} %get-tuple-element.124.weights, f32[24,56,128]{2,1,0:T(8,128)S(1)} %get-tuple-element.91.extended, f32[20,56,128]{2,1,0:T(8,128)S(1)} %get-tuple-element.111.grad_x, f32[20,56,128]{2,1,0:T(8,128)S(1)} %get-tuple-element.112.grad_y), custom_call_target="tpu_custom_call" | custom-call | tf_op jit(solution)/shard_map/pallas_call | solution.py:658
  48.8 2.3 %collective-permute-done.9 = f32[120,128]{1,0:T(8,128)S(1)} collective-permute-done((f32[120,128]{1,0:T(8,128)S(1)}, f32[120,128]{1,0:T(8,128)S(1)}, u32[]{:S(2)}, u32[]{:S(2)}) %collective-permute-start.9) | collective-permute-done | bytes 61472 | tf_op jit(solution)/shard_map/ppermute | solution.py:480
  51.1 0.7 %collective-permute-start.10 = (f32[120,128]{1,0:T(8,128)S(1)}, f32[120,128]{1,0:T(8,128)S(1)}, u32[]{:S(2)}, u32[]{:S(2)}) collective-permute-start(f32[120,128]{1,0:T(8,128)S(1)} %add.113), channel_id=1, source_target_pairs={{0,2},{1,3},{2,0},{3,1},{4,6},{5,7},{6,4},{7,5},{8,10},{9,11},{10,... | collective-permute-start | bytes 184328 | tf_op jit(solution)/shard_map/ppermute | solution.py:480
  51.8 1.9 %shard_map.107 = f32[6,48,128]{2,1,0:T(8,128)S(1)} custom-call(bf16[96,1280]{1,0:T(8,128)(2,1)S(1)} %get-tuple-element.124.weights, f32[24,56,128]{2,1,0:T(8,128)S(1)} %get-tuple-element.91.extended, f32[20,56,128]{2,1,0:T(8,128)S(1)} %get-tuple-element.111.grad_x, f32[20,56,128]{2,1,0:T(8,128)S(1)} %get-tuple-element.112.grad_y), custom_call_target="tpu_custom_call" | custom-call | tf_op jit(solution)/shard_map/pallas_call | solution.py:658
  53.7 1.7 %collective-permute-done.10 = f32[120,128]{1,0:T(8,128)S(1)} collective-permute-done((f32[120,128]{1,0:T(8,128)S(1)}, f32[120,128]{1,0:T(8,128)S(1)}, u32[]{:S(2)}, u32[]{:S(2)}) %collective-permute-start.10) | collective-permute-done | bytes 61472 | tf_op jit(solution)/shard_map/ppermute | solution.py:480
  55.4 0.1 collective-permute-start.11
  55.5 0.5 shard_map.108.moved_ring
  56.0 0.5 shard_map.109.base
  56.5 2.8 %collective-permute-done.11 = f32[120,128]{1,0:T(8,128)S(1)} collective-permute-done((f32[120,128]{1,0:T(8,128)S(1)}, f32[120,128]{1,0:T(8,128)S(1)}, u32[]{:S(2)}, u32[]{:S(2)}) %collective-permute-start.11) | collective-permute-done | bytes 61472 | tf_op jit(solution)/shard_map/ppermute | solution.py:480
  59.3 0.1 collective-permute-start.12
  59.4 1.3 %collective-permute-done.12 = f32[240,128]{1,0:T(8,128)S(1)} collective-permute-done((f32[240,128]{1,0:T(8,128)S(1)}, f32[240,128]{1,0:T(8,128)S(1)}, u32[]{:S(2)}, u32[]{:S(2)}) %collective-permute-start.12) | collective-permute-done | bytes 122912 | tf_op jit(solution)/shard_map/ppermute | solution.py:480
  60.8 1.7 %shard_map.110 = (f32[768,128]{1,0:T(8,128)}, f32[48,128]{1,0:T(8,128)}) custom-call(f32[480,128]{1,0:T(8,128)S(1)} %pad_maximum_fusion.3.tensor, bf16[96,1280]{1,0:T(8,128)(2,1)S(1)} %get-tuple-element.124.weights, bf16[2560,128]{1,0:T(8,128)(2,1)S(1)} %get-tuple-element.127.pieces, f32[48,48]{1,0:T(8,128)S(1)} %get-tuple-element.128.gram_inverse, ...), custom_call_target="tpu_custom_call" | custom-call | tf_op jit(solution)/shard_map/pallas_call | solution.py:686
  (48 shorter events, 0.5 us)
Async XLA Ops:
  0.6 0.7 %copy-start.2 = (s32[128,48]{0,1:T(8,128)S(1)}, s32[128,48]{0,1:T(8,128)}, u32[]{:S(2)}) copy-start(s32[128,48]{0,1:T(8,128)} %param.10) | copy-start | bytes 73732
  0.7 0.7 %copy-start.3 = (f32[2,8,128]{2,1,0:T(8,128)S(1)}, f32[2,8,128]{2,1,0:T(8,128)}, u32[]{:S(2)}) copy-start(f32[2,8,128]{2,1,0:T(8,128)} %param.9) | copy-start | bytes 24580
  0.7 0.7 %copy-start.6 = (s32[8,128]{1,0:T(8,128)S(1)}, s32[8,128]{1,0:T(8,128)}, u32[]{:S(2)}) copy-start(s32[8,128]{1,0:T(8,128)} %water.1) | copy-start | bytes 12292
  0.7 0.7 %copy-start.7 = (f32[48]{0:T(128)S(1)}, f32[48]{0:T(128)}, u32[]{:S(2)}) copy-start(f32[48]{0:T(128)} %param.11) | copy-start | bytes 580
  1.4 1.0 %copy-start = (f32[48,2,8,128]{3,2,1,0:T(8,128)S(1)}, f32[48,2,8,128]{3,2,1,0:T(8,128)}, u32[]{:S(2)}) copy-start(f32[48,2,8,128]{3,2,1,0:T(8,128)} %param.8) | copy-start | bytes 1179652
  3.7 1.7 %collective-permute-start = (f32[488,128]{1,0:T(8,128)S(1)}, f32[488,128]{1,0:T(8,128)S(1)}, u32[]{:S(2)}, u32[]{:S(2)}) collective-permute-start(f32[488,128]{1,0:T(8,128)S(1)} %pad_maximum_fusion.1), channel_id=1, source_target_pairs={{0,8},{8,0},{16,24},{24,16},{1,9},{9,1},{17,25},{25,17},{2,10},{10... | collective-permute-start | bytes 749576 | tf_op jit(solution)/shard_map/ppermute | solution.py:480
  5.5 7.5 %collective-permute-start.1 = (f32[368,128]{1,0:T(8,128)S(1)}, f32[368,128]{1,0:T(8,128)S(1)}, u32[]{:S(2)}, u32[]{:S(2)}) collective-permute-start(f32[368,128]{1,0:T(8,128)S(1)} %pad_maximum_fusion.4), channel_id=1, source_target_pairs={{0,24},{8,16},{16,8},{24,0},{1,25},{9,17},{17,9},{25,1},{2,26},{10... | collective-permute-start | bytes 565256 | tf_op jit(solution)/shard_map/ppermute | solution.py:480
  13.2 5.4 %collective-permute-start.2 = (f32[200,128]{1,0:T(8,128)S(1)}, f32[200,128]{1,0:T(8,128)S(1)}, u32[]{:S(2)}, u32[]{:S(2)}) collective-permute-start(f32[200,128]{1,0:T(8,128)S(1)} %pad_maximum_fusion.8), channel_id=1, source_target_pairs={{0,1},{1,0},{2,3},{3,2},{4,5},{5,4},{6,7},{7,6},{8,9},{9,8},{10,11... | collective-permute-start | bytes 307208 | tf_op jit(solution)/shard_map/ppermute | solution.py:480
  18.6 7.5 %collective-permute-start.3 = (f32[200,128]{1,0:T(8,128)S(1)}, f32[200,128]{1,0:T(8,128)S(1)}, u32[]{:S(2)}, u32[]{:S(2)}) collective-permute-start(f32[200,128]{1,0:T(8,128)S(1)} %pad_maximum_fusion.9), channel_id=1, source_target_pairs={{0,7},{1,2},{2,1},{3,4},{4,3},{5,6},{6,5},{7,0},{8,15},{9,10},{10,... | collective-permute-start | bytes 307208 | tf_op jit(solution)/shard_map/ppermute | solution.py:480
  26.2 5.5 %collective-permute-start.4 = (f32[144,128]{1,0:T(8,128)S(1)}, f32[144,128]{1,0:T(8,128)S(1)}, u32[]{:S(2)}, u32[]{:S(2)}) collective-permute-start(f32[144,128]{1,0:T(8,128)S(1)} %pad_maximum_fusion.10), channel_id=1, source_target_pairs={{0,4},{1,5},{2,6},{3,7},{4,0},{5,1},{6,2},{7,3},{8,12},{9,13},{10,... | collective-permute-start | bytes 221192 | tf_op jit(solution)/shard_map/ppermute | solution.py:480
  31.7 1.4 %collective-permute-start.5 = (f32[240,128]{1,0:T(8,128)S(1)}, f32[240,128]{1,0:T(8,128)S(1)}, u32[]{:S(2)}, u32[]{:S(2)}) collective-permute-start(f32[240,128]{1,0:T(8,128)S(1)} %slice_select_fusion), channel_id=1, source_target_pairs={{0,8},{8,0},{16,24},{24,16},{1,9},{9,1},{17,25},{25,17},{2,10},{10... | collective-permute-start | bytes 368648 | tf_op jit(solution)/shard_map/ppermute | solution.py:480
  33.2 1.4 %copy-start.1 = (f32[1,1280]{1,0:T(1,128)S(1)}, f32[1,1280]{1,0:T(1,128)}, u32[]{:S(2)}) copy-start(f32[1,1280]{1,0:T(1,128)} %constant.71.clone.share) | copy-start | bytes 15364
  33.2 1.4 %copy-start.4 = (s32[1,1280]{1,0:T(1,128)S(1)}, s32[1,1280]{1,0:T(1,128)}, u32[]{:S(2)}) copy-start(s32[1,1280]{1,0:T(1,128)} %constant.70.clone.second) | copy-start | bytes 15364
  33.2 1.4 %copy-start.5 = (s32[1,1280]{1,0:T(1,128)S(1)}, s32[1,1280]{1,0:T(1,128)}, u32[]{:S(2)}) copy-start(s32[1,1280]{1,0:T(1,128)} %constant.69.clone.first) | copy-start | bytes 15364
  33.2 5.7 %collective-permute-start.6 = (f32[240,128]{1,0:T(8,128)S(1)}, f32[240,128]{1,0:T(8,128)S(1)}, u32[]{:S(2)}, u32[]{:S(2)}) collective-permute-start(f32[240,128]{1,0:T(8,128)S(1)} %pad_maximum_fusion.5), channel_id=1, source_target_pairs={{0,24},{8,16},{16,8},{24,0},{1,25},{9,17},{17,9},{25,1},{2,26},{10... | collective-permute-start | bytes 368648 | tf_op jit(solution)/shard_map/ppermute | solution.py:480
  38.9 1.4 %collective-permute-start.7 = (f32[240,128]{1,0:T(8,128)S(1)}, f32[240,128]{1,0:T(8,128)S(1)}, u32[]{:S(2)}, u32[]{:S(2)}) collective-permute-start(f32[240,128]{1,0:T(8,128)S(1)} %pad_maximum_fusion.6), channel_id=1, source_target_pairs={{0,8},{8,0},{16,24},{24,16},{1,9},{9,1},{17,25},{25,17},{2,10},{10... | collective-permute-start | bytes 368648 | tf_op jit(solution)/shard_map/ppermute | solution.py:480
  40.4 6.4 %collective-permute-start.8 = (f32[120,128]{1,0:T(8,128)S(1)}, f32[120,128]{1,0:T(8,128)S(1)}, u32[]{:S(2)}, u32[]{:S(2)}) collective-permute-start(f32[120,128]{1,0:T(8,128)S(1)} %get-tuple-element.104), channel_id=1, source_target_pairs={{0,4},{1,5},{2,6},{3,7},{4,0},{5,1},{6,2},{7,3},{8,12},{9,13},{10,... | collective-permute-start | bytes 184328 | tf_op jit(solution)/shard_map/ppermute | solution.py:480
  46.8 4.3 %collective-permute-start.9 = (f32[120,128]{1,0:T(8,128)S(1)}, f32[120,128]{1,0:T(8,128)S(1)}, u32[]{:S(2)}, u32[]{:S(2)}) collective-permute-start(f32[120,128]{1,0:T(8,128)S(1)} %add.112), channel_id=1, source_target_pairs={{0,1},{1,0},{2,3},{3,2},{4,5},{5,4},{6,7},{7,6},{8,9},{9,8},{10,11... | collective-permute-start | bytes 184328 | tf_op jit(solution)/shard_map/ppermute | solution.py:480
  51.1 4.3 %collective-permute-start.10 = (f32[120,128]{1,0:T(8,128)S(1)}, f32[120,128]{1,0:T(8,128)S(1)}, u32[]{:S(2)}, u32[]{:S(2)}) collective-permute-start(f32[120,128]{1,0:T(8,128)S(1)} %add.113), channel_id=1, source_target_pairs={{0,2},{1,3},{2,0},{3,1},{4,6},{5,7},{6,4},{7,5},{8,10},{9,11},{10,... | collective-permute-start | bytes 184328 | tf_op jit(solution)/shard_map/ppermute | solution.py:480
  55.4 3.9 %collective-permute-start.11 = (f32[120,128]{1,0:T(8,128)S(1)}, f32[120,128]{1,0:T(8,128)S(1)}, u32[]{:S(2)}, u32[]{:S(2)}) collective-permute-start(f32[120,128]{1,0:T(8,128)S(1)} %add.114), channel_id=1, source_target_pairs={{0,24},{8,16},{16,8},{24,0},{1,25},{9,17},{17,9},{25,1},{2,26},{10... | collective-permute-start | bytes 184328 | tf_op jit(solution)/shard_map/ppermute | solution.py:480
  59.3 1.4 %collective-permute-start.12 = (f32[240,128]{1,0:T(8,128)S(1)}, f32[240,128]{1,0:T(8,128)S(1)}, u32[]{:S(2)}, u32[]{:S(2)}) collective-permute-start(f32[240,128]{1,0:T(8,128)S(1)} %pad_maximum_fusion.7), channel_id=1, source_target_pairs={{0,8},{8,0},{16,24},{24,16},{1,9},{9,1},{17,25},{25,17},{2,10},{10... | collective-permute-start | bytes 368648 | tf_op jit(solution)/shard_map/ppermute | solution.py:480
where the time goes:
time: 62.7 us; the launch traced here: 62.5 us
  Pallas kernels  24 us (38%)
  waiting for transfers between devices  20.2 us (32%)
  starting transfers between devices  15 us (24%)
  local copies, waits for them, and re-layouts  1.7 us (3%)
  between operations  1.08 us (2%)
    ppermute x13, waiting for transfers between devices, swap(): return lax.ppermute(values, axis, list(enumerate(partner)))  20.2 us
    ppermute x13, starting transfers between devices, swap(): return lax.ppermute(values, axis, list(enumerate(partner)))  15 us
    pallas_call x3, Pallas kernels, forcing(): call(functools.partial(forcing_kernel, start), out_shape=shape32(2 * (sto...  6.43 us
    pallas_call x3, Pallas kernels, tensor_piece(): call(functools.partial(tensor_kernel, scale, start, stop), out_shape=shap...  6.01 us
    pallas_call x1, Pallas kernels, on_device(): call(functools.partial(inverse_kernel, row_total), out_shape=(shape32(cou...  4.31 us
    pallas_call x1, Pallas kernels, on_device(): call(finish_kernel, out_shape=(shape32(count * 2 * nx, ny), shape32(count...  1.72 us
    unnamed x16, local copies, waits for them, and re-layouts  1.7 us
    pallas_call x1, Pallas kernels, on_device(): call(functools.partial(edge_tensor_kernel, scale), out_shape=shape32(tile...  1.32 us
  transfers between devices with their start and end apart: 13, of which 12 were waited for; matrix products, arithmetic and copies ran while one was open for 0% of the time, Pallas kernels for 33%

commit v1 on v0

--- a/solution.py
+++ b/solution.py
@@ -118,12 +118,11 @@
 
 
 def front_kernel(
-    scale, modes, flow, water, seeds, strength, amplitudes, planes, col_first, col_last, sums, early, coeffs, rows
+    scale, modes, flow, water, seeds, strength, amplitudes, planes, sums, early, coeffs, rows
 ):
     step = coeffs.shape[0]
     total = modes.shape[0] // step
     nx = total // 2
-    fields = planes.shape[1]
     planes[...] = jnp.zeros(planes.shape, jnp.float32)
     diagonal = lax.broadcasted_iota(jnp.int32, (step, step), 0) == lax.broadcasted_iota(jnp.int32, (step, step), 1)
     heights = jnp.sum(jnp.where(diagonal, amplitudes[...], 0.0), axis=1, keepdims=True)
@@ -137,9 +136,6 @@
     tiles = moments.shape[1] // LANES
     for tile in range(tiles):
         sums[tile * step : (tile + 1) * step, :] = moments[:, tile * LANES : (tile + 1) * LANES]
-    ids = lane_ids(fields)
-    first = jnp.zeros((fields, LANES), jnp.float32)
-    last = jnp.zeros((fields, LANES), jnp.float32)
     gram = jnp.zeros((step, step), jnp.float32)
     for x in range(nx):
         mask = water[x : x + 1, :].astype(jnp.float32)
@@ -151,16 +147,9 @@
             planes[q + 4, 0:step, :] = field
             planes[q + 4, step : step + 1, :] = flow[c * nx + x : c * nx + x + 1, :]
             planes[q + 4, step + 1 : step + 2, :] = mask
-            plane = planes[q + 4]
-            first = put_lane(first, ids, plane, 0, q + 2)
-            first = put_lane(first, ids, plane, 1, q + 2 + SECOND)
-            last = put_lane(last, ids, plane, LANES - 1, q + 2)
-            last = put_lane(last, ids, plane, LANES - 2, q + 2 + SECOND)
         wide = jnp.concatenate(both, axis=1)
         weight = jnp.concatenate([mask, mask], axis=1) * scale
         gram += dot_halves(stacked_halves(wide * weight), wide, NT)
-    col_first[...] = first
-    col_last[...] = last
     heads = lax.broadcasted_iota(jnp.int32, (step, step), 0)
     lanes = lax.broadcasted_iota(jnp.int32, (step, step), 1)
     both = jnp.where(lanes < heads, gram, moments[:, pairs : pairs + step])
@@ -183,28 +172,36 @@
     total = planes.shape[0]
     fields = planes.shape[1]
     ids = lane_ids(fields)
-    extended[0:4] = above[...]
-    extended[4 : total - 4] = planes[4 : total - 4]
-    extended[total - 4 :] = below[...]
+    extended[...] = planes[...]
+    extended[2:4] = above[...]
+    extended[total - 4 : total - 2] = below[...]
     first = first_in[...]
     last = last_in[...]
     for c in range(2):
-        for plane, lane in ((above[2 + c], c), (below[c], total - 6 + c)):
+        for plane, lane in ((above[c], c), (below[c], total - 6 + c)):
             first = put_lane(first, ids, plane, 0, lane)
             last = put_lane(last, ids, plane, LANES - 1, lane)
     col_first[...] = first
     col_last[...] = last
 
 
-def plain_gradient_kernel(planes, grad_x, grad_y):
+def plain_gradient_kernel(planes, grad_x, grad_y, col_first, col_last):
     fields = planes.shape[1]
     ids = lane_ids(fields)
+    first = jnp.zeros((fields, LANES), jnp.float32)
+    last = jnp.zeros((fields, LANES), jnp.float32)
     for q in range(grad_x.shape[0]):
         grad_x[q] = 0.5 * (planes[q + 6] - planes[q + 2])
         plane = planes[q + 4]
         east = jnp.where(ids == LANES - 1, 0.0, pltpu.roll(plane, LANES - 1, 1))
         west = jnp.where(ids == 0, 0.0, pltpu.roll(plane, 1, 1))
         grad_y[q] = 0.5 * (east - west)
+        first = put_lane(first, ids, plane, 0, q + 2)
+        first = put_lane(first, ids, plane, 1, q + 2 + SECOND)
+        last = put_lane(last, ids, plane, LANES - 1, q + 2)
+        last = put_lane(last, ids, plane, LANES - 2, q + 2 + SECOND)
+    col_first[...] = first
+    col_last[...] = last
 
 
 def odd_even(packed, ids):
@@ -363,7 +360,7 @@
     return both
 
 
-def inverse_kernel(realizations, early, first, second, share, cov_inverse, gram_inverse, mean, pair_cov, offset):
+def offset_kernel(realizations, early, first, second, share, both, mean, pair_cov, offset):
     count, padded = offset.shape
     packed = jnp.concatenate([early[:, 0:SIDE], early[:, SIDE : 2 * SIDE]], axis=0)
     shared = packed[:, 0:count]
@@ -376,7 +373,8 @@
     gram = jnp.where(col_ids == row_ids, packed[:, count + 1 : count + 2], gram)
     mean_row = jnp.sum(jnp.where(row_ids == col_ids, means, 0.0), axis=0, keepdims=True)
     covariance = raw_second - means * mean_row
-    cov_inverse[...], gram_inverse[...] = inverse_pair(covariance, gram)
+    both[0] = covariance
+    both[1] = gram
     ids = lax.broadcasted_iota(jnp.int32, (count, padded), 0)
     pick_first = (ids == first[...]).astype(jnp.float32)
     pick_second = (ids == second[...]).astype(jnp.float32)
@@ -388,6 +386,10 @@
     offset[...] = means * (cov_pair + mean_first * mean_second) + mean_first * cov_second + mean_second * cov_first
     mean[...] = jnp.broadcast_to(means, mean.shape)
     pair_cov[...] = cov_pair * share[...]
+
+
+def inverse_kernel(both, cov_inverse, gram_inverse):
+    cov_inverse[...], gram_inverse[...] = inverse_pair(both[0], both[1])
 
 
 def weight_kernel(realizations, sums, cov_inverse, offset, share, coeffs, mean, weights, pieces, rows):
@@ -423,11 +425,29 @@
     lax.fori_loop(0, out.shape[0] // 2, body, 0)
 
 
-def ring_forcing_kernel(weights, ring, out, rows):
+def ring_forcing_kernel(weights, extended, far_above, far_below, grad_y, ring, out_rows, out, edge_x, rows):
     count = weights.shape[0] // 2
+    total = extended.shape[0]
     clear_rest(rows, count)
+    stack = weights[...]
+    for c in range(2):
+        edge_x[c] = 0.5 * (extended[4 + c] - far_above[c])
+        edge_x[2 + c] = 0.5 * (far_below[c] - extended[total - 6 + c])
+
+    def body(n, carry):
+        q = n * (total - 6)
+        velocity = [extended.at[q + 2], extended.at[q + 3]]
+        fill_pair_fields(velocity, [(edge_x.at[2 * n + c], grad_y.at[q + c]) for c in range(2)], rows)
+        nonlinear = dot_halves(stack, rows[...], NN)
+        water = extended[q + 2, count + 1 : count + 2, :]
+        for c in range(2):
+            part = nonlinear[:, c * LANES : (c + 1) * LANES]
+            out_rows[2 * n + c] = water * (extended[q + 2 + c, 0:count, :] - TIME_STEP * part)
+        return carry
+
+    lax.fori_loop(0, 2, body, 0)
     fill_pair_fields([ring.at[0], ring.at[1]], [(ring.at[2], ring.at[3])], rows)
-    nonlinear = dot_halves(weights[...], rows[...], NN)
+    nonlinear = dot_halves(stack, rows[:, :LANES], NN)
     out[...] = ring[4, count + 1 : count + 2, :] * (ring[4, 0:count, :] - TIME_STEP * nonlinear)
 
 
@@ -553,11 +573,11 @@
     first_row = lax.axis_index(("row", "col")) * rows_dev
     row_ids = (first_row + jnp.arange(rows_dev, dtype=jnp.int32)).astype(jnp.float32)
     strength = (0.5 + row_ids / row_total).reshape(1, rows_dev)
-    planes, own_first, own_last, sums, early, coeffs = call(
+    planes, sums, early, coeffs = call(
         functools.partial(front_kernel, scale),
         out_shape=(
-            shape32(total, fields, ny), shape32(fields, ny), shape32(fields, ny),
-            shape32(tiles * count, LANES), shape32(count // 2, LANES), shape32(count, rows_dev),
+            shape32(total, fields, ny), shape32(tiles * count, LANES), shape32(count // 2, LANES),
+            shape32(count, rows_dev),
         ),
         scratch_shapes=[vmem32(padded, rows_dev)],
     )(
@@ -565,8 +585,11 @@
         strength, amplitudes.reshape(1, count),
     )
 
-    grads = call(
-        plain_gradient_kernel, out_shape=(shape32(2 * nx, fields, ny), shape32(2 * nx, fields, ny))
+    *grads, own_first, own_last = call(
+        plain_gradient_kernel,
+        out_shape=(
+            shape32(2 * nx, fields, ny), shape32(2 * nx, fields, ny), shape32(fields, ny), shape32(fields, ny),
+        ),
     )(planes)
 
     def tensor_piece(number, grads, *before):
@@ -577,7 +600,8 @@
             scratch_shapes=[vmem32(padded, 2 * ny)],
         )(planes, *grads, *before)
 
-    top, bottom = planes[4:8], planes[total - 8 : total - 4]
+    near_top, far_top = planes[4:6], planes[6:8]
+    far_bottom, near_bottom = planes[total - 8 : total - 6], planes[total - 6 : total - 4]
     row, col = lax.axis_index("row"), lax.axis_index("col")
     even_row, even_col = row % 2 == 0, col % 2 == 0
     lower_a, lower_b = (row + 1) // 2 % 2 == 0, row % 2 == 1
@@ -585,11 +609,23 @@
     col_a, col_b = pairs_a("col"), shifted("col", 1)
 
     kept, sent = split(sums, lower_a)
-    arrived, extra, row_from_a = with_edges("row", row_a, sent, early[None], jnp.where(even_row, bottom, top))
-    kept, early, grads = tied(kept + arrived, early + extra[0], grads)
+    by_way = lax.axis_size("row") == 4
+    far_out = jnp.where(even_row, far_top, far_bottom)
+    arrived, extra, near_a, far_a, *far_way = with_edges(
+        "row", row_a, sent, early[None],
+        jnp.where(even_row, near_bottom, near_top), jnp.where(even_row, far_bottom, far_top),
+        *([far_out] if by_way else []),
+    )
+    kept, early, own_first, *grads = tied(kept + arrived, early + extra[0], own_first, *grads)
+    near_out = jnp.where(even_row, near_top, near_bottom)
+    if by_way:
+        outer = (row == 0) | (row == lax.axis_size("row") - 1)
+        edges_out = [jnp.where(outer, far_way[0], near_out)]
+    else:
+        edges_out = [near_out, far_out]
     kept, sent = split(kept, lower_b)
-    arrived, extra, row_from_b = with_edges("row", row_b, sent, early[None], jnp.where(even_row, top, bottom))
-    above, below = neighbours("row", row_from_a, row_from_b)
+    arrived, extra, near_b, *far_b = with_edges("row", row_b, sent, early[None], *edges_out)
+    above, below = neighbours("row", near_a, near_b)
     tensor = tensor_piece(0, grads)
     kept, early, above, below, tensor = tied(kept + arrived, early + extra[0], above, below, tensor)
     extended, col_first, col_last = call(
@@ -626,19 +662,23 @@
     moments = kept
 
     kept, sent = split(tensor, lower_a)
-    kept, moments = tied(kept + swap(sent, "row", row_a), moments)
+    arrived, *far_way = with_edges("row", row_a, sent, *([near_b] if by_way else []))
+    far_above, far_below = neighbours("row", far_a, (far_way if by_way else far_b)[0])
+    both, mean, pair_cov, offset = call(
+        functools.partial(offset_kernel, row_total),
+        out_shape=(
+            shape32(2, count, count), shape32(count, rows_dev), shape32(1, padded), shape32(count, padded),
+        ),
+    )(early, first, second, share)
+    kept, moments, both, far_above = tied(kept + arrived, moments, both, far_above)
     kept, sent = split(kept, lower_b)
     arrived, other = with_edges("row", row_b, sent, moments[None])
     kept = kept + arrived
-    cov_inverse, gram_inverse, mean, pair_cov, offset = call(
-        functools.partial(inverse_kernel, row_total),
-        out_shape=(
-            shape32(count, count), shape32(count, count), shape32(count, rows_dev), shape32(1, padded),
-            shape32(count, padded),
-        ),
-    )(early, first, second, share)
+    cov_inverse, gram_inverse = call(
+        inverse_kernel, out_shape=(shape32(count, count), shape32(count, count))
+    )(both)
     moments = joined(moments, other[0], lower_b)
-    kept, moments, offset = tied(kept, moments, offset)
+    kept, moments, cov_inverse = tied(kept, moments, cov_inverse)
     sums = joined(moments, swap(moments, "row", row_a), lower_a)
     kept, sums = tied(kept, sums)
     weights, pieces = call(
@@ -651,7 +691,7 @@
     )(sums, cov_inverse, offset, share, coeffs, mean)
     col_bits = axis_bits("col")
     steps = later_steps("row") + [
-        ("col", [i ^ (1 << bit) for i in range(lax.axis_size("col"))]) for bit in col_bits[-1:] + col_bits[:-1]
+        ("col", [i ^ (1 << bit) for i in range(lax.axis_size("col"))]) for bit in col_bits
     ]
 
     def forcing(start, stop):
@@ -662,12 +702,13 @@
         )(weights, extended, grad_x, grad_y)
 
     def ring_forcing():
-        return call(ring_forcing_kernel, out_shape=shape32(count, ny), scratch_shapes=[vmem32(padded, ny)])(
-            weights, ring
-        )
-
-    ends = [(nx + 2) * n // 10 for n in (0, 4, 7, 10)]
-    works = [functools.partial(forcing, ends[n], ends[n + 1]) for n in range(3)] + [ring_forcing]
+        return call(
+            ring_forcing_kernel,
+            out_shape=(shape32(4, count, ny), shape32(count, ny)),
+            scratch_shapes=[vmem32(4, fields, ny), vmem32(padded, 2 * ny)],
+        )(weights, extended, far_above, far_below, grad_y, ring)
+
+    works = [functools.partial(forcing, 1 + nx * n // 2, 1 + nx * (n + 1) // 2) for n in range(2)] + [ring_forcing]
     moved = []
     for axis, partner in steps:
         total_kept = kept + swap(kept, axis, partner)
@@ -677,8 +718,9 @@
     kept = joined(kept, swap(kept, "row", row_b), lower_b)
     while works:
         moved.append(works.pop(0)())
+    moved_rows, moved_ring = moved.pop()
     base = call(smooth_kernel, out_shape=shape32(2 * nx, count, ny))(
-        extended, jnp.concatenate(moved[:-1], axis=0), moved[-1]
+        extended, jnp.concatenate([moved_rows[:2], *moved, moved_rows[2:]], axis=0), moved_ring
     )
     kept, base = tied(kept, base)
     tensor = joined(kept, swap(kept, "row", row_a), lower_a)

time: 62.7 us -> 61.4 us (0.979)
  waiting for transfers between devices: 20.2 us -> 13.3 us
  starting transfers between devices: 15 us -> 18.7 us
  Pallas kernels: 24 us -> 25.2 us
    ppermute x13, waiting for transfers between devices: 20.2 us -> 13.3 us  [swap(): return lax.ppermute(values, axis, list(enumerate(partner)))]
    ppermute x13, starting transfers between devices: 15 us -> 18.7 us  [swap(): return lax.ppermute(values, axis, list(enumerate(partner)))]
    pallas_call x2 -> x3, Pallas kernels: 4.78 us -> 6.61 us  [the longest x1 4.07 us: on_device(): call(inverse_kernel, out_shape=(shape32(count, count), shape32(count, cou...]
    pallas_call x3 -> x2, Pallas kernels: 6.43 us -> 5.33 us  [forcing(): call(functools.partial(forcing_kernel, start), out_shape=shape32(2 * (sto...]
    unnamed x16 -> x19, local copies, waits for them, and re-layouts: 1.7 us -> 2.29 us
  transfers between devices with their start and end apart: 13 -> 13, of which waited for: 12 -> 11; matrix products, arithmetic and copies ran while one was open for 0% -> 0% of each run, Pallas kernels for 33% -> 36%
where the time goes in v1:
time: 61.4 us; the launch traced here: 61.1 us
  Pallas kernels  25.2 us (41%)
  starting transfers between devices  18.7 us (30%)
  waiting for transfers between devices  13.3 us (22%)
  local copies, waits for them, and re-layouts  2.31 us (4%)
  between operations  1.14 us (2%)
    ppermute x13, starting transfers between devices, swap(): return lax.ppermute(values, axis, list(enumerate(partner)))  18.7 us
    ppermute x13, waiting for transfers between devices, swap(): return lax.ppermute(values, axis, list(enumerate(partner)))  13.3 us
    pallas_call x3, Pallas kernels, tensor_piece(): call(functools.partial(tensor_kernel, scale, start, stop), out_shape=shap...  6.01 us
    pallas_call x2, Pallas kernels, forcing(): call(functools.partial(forcing_kernel, start), out_shape=shape32(2 * (sto...  5.33 us
    pallas_call x1, Pallas kernels, on_device(): call(inverse_kernel, out_shape=(shape32(count, count), shape32(count, cou...  4.07 us
    unnamed x19, local copies, waits for them, and re-layouts  2.29 us
    pallas_call x1, Pallas kernels, ring_forcing(): call(ring_forcing_kernel, out_shape=(shape32(4, count, ny), shape32(count...  1.84 us
    pallas_call x1, Pallas kernels, on_device(): call(finish_kernel, out_shape=(shape32(count * 2 * nx, ny), shape32(count...  1.72 us
  transfers between devices with their start and end apart: 13, of which 11 were waited for; matrix products, arithmetic and copies ran while one was open for 0% of the time, Pallas kernels for 36%

profile of v1, /device:TPU:0, one launch (start us, length us, event | category | flops | bytes accessed | tf_op | source)
XLA Modules:
  0.0 61.1 jit_solution(2471197572186731722)
XLA Ops:
  0.7 0.7 %copy-done.2 = s32[128,48]{0,1:T(8,128)S(1)} copy-done((s32[128,48]{0,1:T(8,128)S(1)}, s32[128,48]{0,1:T(8,128)}, u32[]{:S(2)}) %copy-start.2) | copy-done | bytes 24600
  1.4 0.0 copy-done.6
  1.4 1.0 %copy-done = f32[48,2,8,128]{3,2,1,0:T(8,128)S(1)} copy-done((f32[48,2,8,128]{3,2,1,0:T(8,128)S(1)}, f32[48,2,8,128]{3,2,1,0:T(8,128)}, u32[]{:S(2)}) %copy-start) | copy-done | bytes 393240
  2.4 1.2 %shard_map.95 = (f32[24,56,128]{2,1,0:T(8,128)S(1)}, f32[480,128]{1,0:T(8,128)S(1)}, f32[24,128]{1,0:T(8,128)S(1)}, f32[48,128]{1,0:T(8,128)S(1)}) custom-call(f32[768,128]{1,0:T(8,128)S(1)} %bitcast.15, f32[16,128]{1,0:T(8,128)S(1)} %bitcast.21, s32[8,128]{1,0:T(8,128)S(1)} %copy-done.6, s32[48,128]{1,0:T(8,128)S(1)} %bitcast.20, ...), custom_call_target="tpu_custom_call" | custom-call | tf_op jit(solution)/shard_map/pallas_call | solution.py:576
  3.7 0.5 collective-permute-start
  4.2 0.8 %shard_map.96 = (f32[16,56,128]{2,1,0:T(8,128)S(1)}, f32[16,56,128]{2,1,0:T(8,128)S(1)}, f32[56,128]{1,0:T(8,128)S(1)}, f32[56,128]{1,0:T(8,128)S(1)}) custom-call(f32[24,56,128]{2,1,0:T(8,128)S(1)} %get-tuple-element.77.planes), custom_call_target="tpu_custom_call" | custom-call | tf_op jit(solution)/shard_map/pallas_call | solution.py:588
  5.0 0.4 collective-permute-done
  5.5 2.7 %collective-permute-start.1 = (f32[256,128]{1,0:T(8,128)S(1)}, f32[256,128]{1,0:T(8,128)S(1)}, u32[]{:S(2)}, u32[]{:S(2)}) collective-permute-start(f32[256,128]{1,0:T(8,128)S(1)} %pad_maximum_fusion.4), channel_id=1, source_target_pairs={{0,24},{8,16},{16,8},{24,0},{1,25},{9,17},{17,9},{25,1},{2,26},{10... | collective-permute-start | bytes 393224 | tf_op jit(solution)/shard_map/ppermute | solution.py:500
  8.2 1.5 %shard_map.97.refs_0_ = f32[480,128]{1,0:T(8,128)S(1)} custom-call(f32[24,56,128]{2,1,0:T(8,128)S(1)} %get-tuple-element.77.planes, f32[16,56,128]{2,1,0:T(8,128)S(1)} %get-tuple-element.83.grad_x, f32[16,56,128]{2,1,0:T(8,128)S(1)} %get-tuple-element.84.grad_y), custom_call_target="tpu_custom_call" | custom-call | tf_op jit(solution)/shard_map/pallas_call | solution.py:597
  9.8 2.1 %collective-permute-done.1 = f32[256,128]{1,0:T(8,128)S(1)} collective-permute-done((f32[256,128]{1,0:T(8,128)S(1)}, f32[256,128]{1,0:T(8,128)S(1)}, u32[]{:S(2)}, u32[]{:S(2)}) %collective-permute-start.1) | collective-permute-done | bytes 131104 | tf_op jit(solution)/shard_map/ppermute | solution.py:500
  11.9 0.2 shard_map.98
  12.1 2.2 %collective-permute-start.2 = (f32[200,128]{1,0:T(8,128)S(1)}, f32[200,128]{1,0:T(8,128)S(1)}, u32[]{:S(2)}, u32[]{:S(2)}) collective-permute-start(f32[200,128]{1,0:T(8,128)S(1)} %pad_maximum_fusion.8), channel_id=1, source_target_pairs={{0,1},{1,0},{2,3},{3,2},{4,5},{5,4},{6,7},{7,6},{8,9},{9,8},{10,11... | collective-permute-start | bytes 307208 | tf_op jit(solution)/shard_map/ppermute | solution.py:500
  14.3 2.2 %shard_map.99.refs_0_ = f32[480,128]{1,0:T(8,128)S(1)} custom-call(f32[24,56,128]{2,1,0:T(8,128)S(1)} %get-tuple-element.77.planes, f32[16,56,128]{2,1,0:T(8,128)S(1)} %get-tuple-element.83.grad_x, f32[16,56,128]{2,1,0:T(8,128)S(1)} %get-tuple-element.84.grad_y, f32[480,128]{1,0:T(8,128)S(1)} %shard_map.97.refs_0_), custom_call_target="tpu_custom_call" | custom-call | tf_op jit(solution)/shard_map/pallas_call | solution.py:597
  16.5 0.9 %collective-permute-done.2 = f32[200,128]{1,0:T(8,128)S(1)} collective-permute-done((f32[200,128]{1,0:T(8,128)S(1)}, f32[200,128]{1,0:T(8,128)S(1)}, u32[]{:S(2)}, u32[]{:S(2)}) %collective-permute-start.2) | collective-permute-done | bytes 102432 | tf_op jit(solution)/shard_map/ppermute | solution.py:500
  17.5 4.8 %collective-permute-start.3 = (f32[200,128]{1,0:T(8,128)S(1)}, f32[200,128]{1,0:T(8,128)S(1)}, u32[]{:S(2)}, u32[]{:S(2)}) collective-permute-start(f32[200,128]{1,0:T(8,128)S(1)} %pad_maximum_fusion.9), channel_id=1, source_target_pairs={{0,7},{1,2},{2,1},{3,4},{4,3},{5,6},{6,5},{7,0},{8,15},{9,10},{10,... | collective-permute-start | bytes 307208 | tf_op jit(solution)/shard_map/ppermute | solution.py:500
  22.3 2.3 %shard_map.100.before = f32[480,128]{1,0:T(8,128)S(1)} custom-call(f32[24,56,128]{2,1,0:T(8,128)S(1)} %get-tuple-element.77.planes, f32[16,56,128]{2,1,0:T(8,128)S(1)} %get-tuple-element.83.grad_x, f32[16,56,128]{2,1,0:T(8,128)S(1)} %get-tuple-element.84.grad_y, f32[480,128]{1,0:T(8,128)S(1)} %shard_map.99.refs_0_), custom_call_target="tpu_custom_call" | custom-call | tf_op jit(solution)/shard_map/pallas_call | solution.py:597
  24.6 0.4 collective-permute-done.3
  25.0 1.0 %collective-permute-start.4 = (f32[144,128]{1,0:T(8,128)S(1)}, f32[144,128]{1,0:T(8,128)S(1)}, u32[]{:S(2)}, u32[]{:S(2)}) collective-permute-start(f32[144,128]{1,0:T(8,128)S(1)} %pad_maximum_fusion.10), channel_id=1, source_target_pairs={{0,4},{1,5},{2,6},{3,7},{4,0},{5,1},{6,2},{7,3},{8,12},{9,13},{10,... | collective-permute-start | bytes 221192 | tf_op jit(solution)/shard_map/ppermute | solution.py:500
  26.1 1.2 %shard_map.102 = (f32[20,56,128]{2,1,0:T(8,128)S(1)}, f32[20,56,128]{2,1,0:T(8,128)S(1)}, f32[5,56,128]{2,1,0:T(8,128)S(1)}, f32[16,48,128]{2,1,0:T(8,128)S(1)}) custom-call(f32[24,56,128]{2,1,0:T(8,128)S(1)} %get-tuple-element.99.extended, f32[56,128]{1,0:T(8,128)S(1)} %get-tuple-element.100.left, f32[56,128]{1,0:T(8,128)S(1)} %get-tuple-element.101.right, ...), custom_call_target="tpu_custom_call" | custom-call | tf_op jit(solution)/shard_map/pallas_call | solution.py:654
  27.2 1.3 %shard_map.101 = f32[480,128]{1,0:T(8,128)S(1)} custom-call(f32[24,56,128]{2,1,0:T(8,128)S(1)} %get-tuple-element.99.extended, f32[56,128]{1,0:T(8,128)S(1)} %get-tuple-element.100.left, f32[56,128]{1,0:T(8,128)S(1)} %get-tuple-element.101.right, f32[56,128]{1,0:T(8,128)S(1)} %get-tuple-element.92.col_first, f32[56,128]{1,0:T(8,128)S(1)} %get-tuple-element.91.col_last, ...), custom_call_target="tpu_custom_call" | custom-call | tf_op jit(solution)/shard_map/pallas_call | solution.py:649
  28.6 2.0 %collective-permute-done.4 = f32[144,128]{1,0:T(8,128)S(1)} collective-permute-done((f32[144,128]{1,0:T(8,128)S(1)}, f32[144,128]{1,0:T(8,128)S(1)}, u32[]{:S(2)}, u32[]{:S(2)}) %collective-permute-start.4) | collective-permute-done | bytes 73760 | tf_op jit(solution)/shard_map/ppermute | solution.py:500
  30.6 0.0 copy-start.1
  30.6 0.0 copy-start.4
  30.6 0.1 collective-permute-start.5
  30.7 0.6 copy-done.1
  31.3 0.0 copy-done.4
  31.3 0.0 copy-done.5
  31.3 0.7 %shard_map.103 = (f32[2,48,48]{2,1,0:T(8,128)S(1)}, f32[48,128]{1,0:T(8,128)S(1)}, f32[1,1280]{1,0:T(1,128)S(1)}, f32[48,1280]{1,0:T(8,128)S(1)}) custom-call(f32[24,128]{1,0:T(8,128)S(1)} %slice_add_fusion.7.early, s32[1,1280]{1,0:T(1,128)S(1)} %copy-done.5, s32[1,1280]{1,0:T(1,128)S(1)} %copy-done.4, f32[1,1280]{1,0:T(1,128)S(1)} %copy-done.1), custom_call_target="tpu_custom_call" | custom-call | tf_op jit(solution)/shard_map/pallas_call | solution.py:667
  32.0 0.1 collective-permute-done.5
  32.2 1.3 %collective-permute-start.6 = (f32[240,128]{1,0:T(8,128)S(1)}, f32[240,128]{1,0:T(8,128)S(1)}, u32[]{:S(2)}, u32[]{:S(2)}) collective-permute-start(f32[240,128]{1,0:T(8,128)S(1)} %pad_maximum_fusion.5), channel_id=1, source_target_pairs={{0,24},{8,16},{16,8},{24,0},{1,25},{9,17},{17,9},{25,1},{2,26},{10... | collective-permute-start | bytes 368648 | tf_op jit(solution)/shard_map/ppermute | solution.py:500
  33.5 4.1 %shard_map.104 = (f32[48,48]{1,0:T(8,128)S(1)}, f32[48,48]{1,0:T(8,128)S(1)}) custom-call(f32[2,48,48]{2,1,0:T(8,128)S(1)} %get-tuple-element.110.both), custom_call_target="tpu_custom_call" | custom-call | tf_op jit(solution)/shard_map/pallas_call | solution.py:677
  37.7 0.4 collective-permute-start.7
  38.1 1.0 %collective-permute-done.7 = f32[240,128]{1,0:T(8,128)S(1)} collective-permute-done((f32[240,128]{1,0:T(8,128)S(1)}, f32[240,128]{1,0:T(8,128)S(1)}, u32[]{:S(2)}, u32[]{:S(2)}) %collective-permute-start.7) | collective-permute-done | bytes 122912 | tf_op jit(solution)/shard_map/ppermute | solution.py:500
  39.1 0.5 collective-permute-start.8
  39.6 0.4 shard_map.105
  40.1 2.7 %shard_map.106 = f32[8,48,128]{2,1,0:T(8,128)S(1)} custom-call(bf16[96,1280]{1,0:T(8,128)(2,1)S(1)} %get-tuple-element.140.weights, f32[24,56,128]{2,1,0:T(8,128)S(1)} %get-tuple-element.99.extended, f32[20,56,128]{2,1,0:T(8,128)S(1)} %get-tuple-element.121.grad_x, f32[20,56,128]{2,1,0:T(8,128)S(1)} %get-tuple-element.122.grad_y), custom_call_target="tpu_custom_call" | custom-call | tf_op jit(solution)/shard_map/pallas_call | solution.py:698
  42.7 0.7 %collective-permute-done.8 = f32[120,128]{1,0:T(8,128)S(1)} collective-permute-done((f32[120,128]{1,0:T(8,128)S(1)}, f32[120,128]{1,0:T(8,128)S(1)}, u32[]{:S(2)}, u32[]{:S(2)}) %collective-permute-start.8) | collective-permute-done | bytes 61472 | tf_op jit(solution)/shard_map/ppermute | solution.py:500
  43.5 2.1 %collective-permute-start.9 = (f32[120,128]{1,0:T(8,128)S(1)}, f32[120,128]{1,0:T(8,128)S(1)}, u32[]{:S(2)}, u32[]{:S(2)}) collective-permute-start(f32[120,128]{1,0:T(8,128)S(1)} %add.113), channel_id=1, source_target_pairs={{0,2},{1,3},{2,0},{3,1},{4,6},{5,7},{6,4},{7,5},{8,10},{9,11},{10,... | collective-permute-start | bytes 184328 | tf_op jit(solution)/shard_map/ppermute | solution.py:500
  45.5 2.7 %shard_map.107 = f32[8,48,128]{2,1,0:T(8,128)S(1)} custom-call(bf16[96,1280]{1,0:T(8,128)(2,1)S(1)} %get-tuple-element.140.weights, f32[24,56,128]{2,1,0:T(8,128)S(1)} %get-tuple-element.99.extended, f32[20,56,128]{2,1,0:T(8,128)S(1)} %get-tuple-element.121.grad_x, f32[20,56,128]{2,1,0:T(8,128)S(1)} %get-tuple-element.122.grad_y), custom_call_target="tpu_custom_call" | custom-call | tf_op jit(solution)/shard_map/pallas_call | solution.py:698
  48.2 2.8 %collective-permute-start.10 = (f32[120,128]{1,0:T(8,128)S(1)}, f32[120,128]{1,0:T(8,128)S(1)}, u32[]{:S(2)}, u32[]{:S(2)}) collective-permute-start(f32[120,128]{1,0:T(8,128)S(1)} %add.114), channel_id=1, source_target_pairs={{0,4},{1,5},{2,6},{3,7},{4,0},{5,1},{6,2},{7,3},{8,12},{9,13},{10,... | collective-permute-start | bytes 184328 | tf_op jit(solution)/shard_map/ppermute | solution.py:500
  51.0 1.8 %shard_map.108 = (f32[4,48,128]{2,1,0:T(8,128)S(1)}, f32[48,128]{1,0:T(8,128)S(1)}) custom-call(bf16[96,1280]{1,0:T(8,128)(2,1)S(1)} %get-tuple-element.140.weights, f32[24,56,128]{2,1,0:T(8,128)S(1)} %get-tuple-element.99.extended, f32[2,56,128]{2,1,0:T(8,128)S(1)} %bitcast.17, f32[2,56,128]{2,1,0:T(8,128)S(1)} %bitcast.16, ...), custom_call_target="tpu_custom_call" | custom-call | tf_op jit(solution)/shard_map/pallas_call | solution.py:705
  52.9 0.8 %collective-permute-done.10 = f32[120,128]{1,0:T(8,128)S(1)} collective-permute-done((f32[120,128]{1,0:T(8,128)S(1)}, f32[120,128]{1,0:T(8,128)S(1)}, u32[]{:S(2)}, u32[]{:S(2)}) %collective-permute-start.10) | collective-permute-done | bytes 61472 | tf_op jit(solution)/shard_map/ppermute | solution.py:500
  53.7 0.1 collective-permute-start.11
  53.8 0.5 shard_map.109.base
  54.3 3.6 %collective-permute-done.11 = f32[120,128]{1,0:T(8,128)S(1)} collective-permute-done((f32[120,128]{1,0:T(8,128)S(1)}, f32[120,128]{1,0:T(8,128)S(1)}, u32[]{:S(2)}, u32[]{:S(2)}) %collective-permute-start.11) | collective-permute-done | bytes 61472 | tf_op jit(solution)/shard_map/ppermute | solution.py:500
  57.9 0.1 collective-permute-start.12
  58.0 1.3 %collective-permute-done.12 = f32[240,128]{1,0:T(8,128)S(1)} collective-permute-done((f32[240,128]{1,0:T(8,128)S(1)}, f32[240,128]{1,0:T(8,128)S(1)}, u32[]{:S(2)}, u32[]{:S(2)}) %collective-permute-start.12) | collective-permute-done | bytes 122912 | tf_op jit(solution)/shard_map/ppermute | solution.py:500
  59.4 1.7 %shard_map.110 = (f32[768,128]{1,0:T(8,128)}, f32[48,128]{1,0:T(8,128)}) custom-call(f32[480,128]{1,0:T(8,128)S(1)} %pad_maximum_fusion.2.tensor, bf16[96,1280]{1,0:T(8,128)(2,1)S(1)} %get-tuple-element.140.weights, bf16[2560,128]{1,0:T(8,128)(2,1)S(1)} %get-tuple-element.141.pieces, f32[48,48]{1,0:T(8,128)S(1)} %get-tuple-element.142.gram_inverse, ...), custom_call_target="tpu_custom_call" | custom-call | tf_op jit(solution)/shard_map/pallas_call | solution.py:728
  (56 shorter events, 0.6 us)
Async XLA Ops:
  0.6 0.7 %copy-start.2 = (s32[128,48]{0,1:T(8,128)S(1)}, s32[128,48]{0,1:T(8,128)}, u32[]{:S(2)}) copy-start(s32[128,48]{0,1:T(8,128)} %param.10) | copy-start | bytes 73732
  0.7 0.7 %copy-start.3 = (f32[2,8,128]{2,1,0:T(8,128)S(1)}, f32[2,8,128]{2,1,0:T(8,128)}, u32[]{:S(2)}) copy-start(f32[2,8,128]{2,1,0:T(8,128)} %param.9) | copy-start | bytes 24580
  0.7 0.7 %copy-start.6 = (s32[8,128]{1,0:T(8,128)S(1)}, s32[8,128]{1,0:T(8,128)}, u32[]{:S(2)}) copy-start(s32[8,128]{1,0:T(8,128)} %water.1) | copy-start | bytes 12292
  0.7 0.7 %copy-start.7 = (f32[48]{0:T(128)S(1)}, f32[48]{0:T(128)}, u32[]{:S(2)}) copy-start(f32[48]{0:T(128)} %param.11) | copy-start | bytes 580
  1.4 1.0 %copy-start = (f32[48,2,8,128]{3,2,1,0:T(8,128)S(1)}, f32[48,2,8,128]{3,2,1,0:T(8,128)}, u32[]{:S(2)}) copy-start(f32[48,2,8,128]{3,2,1,0:T(8,128)} %param.8) | copy-start | bytes 1179652
  3.7 1.7 %collective-permute-start = (f32[600,128]{1,0:T(8,128)S(1)}, f32[600,128]{1,0:T(8,128)S(1)}, u32[]{:S(2)}, u32[]{:S(2)}) collective-permute-start(f32[600,128]{1,0:T(8,128)S(1)} %constant_dynamic-update-slice_fusion), channel_id=1, source_target_pairs={{0,8},{8,0},{16,24},{24,16},{1,9},{9,1},{17,25},{25,17},{2,10},{10... | collective-permute-start | bytes 921608 | tf_op jit(solution)/shard_map/ppermute | solution.py:500
  5.5 6.3 %collective-permute-start.1 = (f32[256,128]{1,0:T(8,128)S(1)}, f32[256,128]{1,0:T(8,128)S(1)}, u32[]{:S(2)}, u32[]{:S(2)}) collective-permute-start(f32[256,128]{1,0:T(8,128)S(1)} %pad_maximum_fusion.4), channel_id=1, source_target_pairs={{0,24},{8,16},{16,8},{24,0},{1,25},{9,17},{17,9},{25,1},{2,26},{10... | collective-permute-start | bytes 393224 | tf_op jit(solution)/shard_map/ppermute | solution.py:500
  12.1 5.4 %collective-permute-start.2 = (f32[200,128]{1,0:T(8,128)S(1)}, f32[200,128]{1,0:T(8,128)S(1)}, u32[]{:S(2)}, u32[]{:S(2)}) collective-permute-start(f32[200,128]{1,0:T(8,128)S(1)} %pad_maximum_fusion.8), channel_id=1, source_target_pairs={{0,1},{1,0},{2,3},{3,2},{4,5},{5,4},{6,7},{7,6},{8,9},{9,8},{10,11... | collective-permute-start | bytes 307208 | tf_op jit(solution)/shard_map/ppermute | solution.py:500
  17.5 7.5 %collective-permute-start.3 = (f32[200,128]{1,0:T(8,128)S(1)}, f32[200,128]{1,0:T(8,128)S(1)}, u32[]{:S(2)}, u32[]{:S(2)}) collective-permute-start(f32[200,128]{1,0:T(8,128)S(1)} %pad_maximum_fusion.9), channel_id=1, source_target_pairs={{0,7},{1,2},{2,1},{3,4},{4,3},{5,6},{6,5},{7,0},{8,15},{9,10},{10,... | collective-permute-start | bytes 307208 | tf_op jit(solution)/shard_map/ppermute | solution.py:500
  25.0 5.5 %collective-permute-start.4 = (f32[144,128]{1,0:T(8,128)S(1)}, f32[144,128]{1,0:T(8,128)S(1)}, u32[]{:S(2)}, u32[]{:S(2)}) collective-permute-start(f32[144,128]{1,0:T(8,128)S(1)} %pad_maximum_fusion.10), channel_id=1, source_target_pairs={{0,4},{1,5},{2,6},{3,7},{4,0},{5,1},{6,2},{7,3},{8,12},{9,13},{10,... | collective-permute-start | bytes 221192 | tf_op jit(solution)/shard_map/ppermute | solution.py:500
  30.6 0.7 %copy-start.1 = (f32[1,1280]{1,0:T(1,128)S(1)}, f32[1,1280]{1,0:T(1,128)}, u32[]{:S(2)}) copy-start(f32[1,1280]{1,0:T(1,128)} %constant.73.clone.share) | copy-start | bytes 15364
  30.6 0.7 %copy-start.4 = (s32[1,1280]{1,0:T(1,128)S(1)}, s32[1,1280]{1,0:T(1,128)}, u32[]{:S(2)}) copy-start(s32[1,1280]{1,0:T(1,128)} %constant.72.clone.second) | copy-start | bytes 15364
  30.6 0.7 %copy-start.5 = (s32[1,1280]{1,0:T(1,128)S(1)}, s32[1,1280]{1,0:T(1,128)}, u32[]{:S(2)}) copy-start(s32[1,1280]{1,0:T(1,128)} %constant.71.clone.first) | copy-start | bytes 15364
  30.6 1.5 %collective-permute-start.5 = (f32[352,128]{1,0:T(8,128)S(1)}, f32[352,128]{1,0:T(8,128)S(1)}, u32[]{:S(2)}, u32[]{:S(2)}) collective-permute-start(f32[352,128]{1,0:T(8,128)S(1)} %pad_maximum_fusion.3), channel_id=1, source_target_pairs={{0,8},{8,0},{16,24},{24,16},{1,9},{9,1},{17,25},{25,17},{2,10},{10... | collective-permute-start | bytes 540680 | tf_op jit(solution)/shard_map/ppermute | solution.py:500
  32.2 5.4 %collective-permute-start.6 = (f32[240,128]{1,0:T(8,128)S(1)}, f32[240,128]{1,0:T(8,128)S(1)}, u32[]{:S(2)}, u32[]{:S(2)}) collective-permute-start(f32[240,128]{1,0:T(8,128)S(1)} %pad_maximum_fusion.5), channel_id=1, source_target_pairs={{0,24},{8,16},{16,8},{24,0},{1,25},{9,17},{17,9},{25,1},{2,26},{10... | collective-permute-start | bytes 368648 | tf_op jit(solution)/shard_map/ppermute | solution.py:500
  37.7 1.4 %collective-permute-start.7 = (f32[240,128]{1,0:T(8,128)S(1)}, f32[240,128]{1,0:T(8,128)S(1)}, u32[]{:S(2)}, u32[]{:S(2)}) collective-permute-start(f32[240,128]{1,0:T(8,128)S(1)} %pad_maximum_fusion.6), channel_id=1, source_target_pairs={{0,8},{8,0},{16,24},{24,16},{1,9},{9,1},{17,25},{25,17},{2,10},{10... | collective-permute-start | bytes 368648 | tf_op jit(solution)/shard_map/ppermute | solution.py:500
  39.1 4.3 %collective-permute-start.8 = (f32[120,128]{1,0:T(8,128)S(1)}, f32[120,128]{1,0:T(8,128)S(1)}, u32[]{:S(2)}, u32[]{:S(2)}) collective-permute-start(f32[120,128]{1,0:T(8,128)S(1)} %get-tuple-element.114), channel_id=1, source_target_pairs={{0,1},{1,0},{2,3},{3,2},{4,5},{5,4},{6,7},{7,6},{8,9},{9,8},{10,11... | collective-permute-start | bytes 184328 | tf_op jit(solution)/shard_map/ppermute | solution.py:500
  43.5 4.7 %collective-permute-start.9 = (f32[120,128]{1,0:T(8,128)S(1)}, f32[120,128]{1,0:T(8,128)S(1)}, u32[]{:S(2)}, u32[]{:S(2)}) collective-permute-start(f32[120,128]{1,0:T(8,128)S(1)} %add.113), channel_id=1, source_target_pairs={{0,2},{1,3},{2,0},{3,1},{4,6},{5,7},{6,4},{7,5},{8,10},{9,11},{10,... | collective-permute-start | bytes 184328 | tf_op jit(solution)/shard_map/ppermute | solution.py:500
  48.2 5.4 %collective-permute-start.10 = (f32[120,128]{1,0:T(8,128)S(1)}, f32[120,128]{1,0:T(8,128)S(1)}, u32[]{:S(2)}, u32[]{:S(2)}) collective-permute-start(f32[120,128]{1,0:T(8,128)S(1)} %add.114), channel_id=1, source_target_pairs={{0,4},{1,5},{2,6},{3,7},{4,0},{5,1},{6,2},{7,3},{8,12},{9,13},{10,... | collective-permute-start | bytes 184328 | tf_op jit(solution)/shard_map/ppermute | solution.py:500
  53.7 4.2 %collective-permute-start.11 = (f32[120,128]{1,0:T(8,128)S(1)}, f32[120,128]{1,0:T(8,128)S(1)}, u32[]{:S(2)}, u32[]{:S(2)}) collective-permute-start(f32[120,128]{1,0:T(8,128)S(1)} %add.115), channel_id=1, source_target_pairs={{0,24},{8,16},{16,8},{24,0},{1,25},{9,17},{17,9},{25,1},{2,26},{10... | collective-permute-start | bytes 184328 | tf_op jit(solution)/shard_map/ppermute | solution.py:500
  57.9 1.4 %collective-permute-start.12 = (f32[240,128]{1,0:T(8,128)S(1)}, f32[240,128]{1,0:T(8,128)S(1)}, u32[]{:S(2)}, u32[]{:S(2)}) collective-permute-start(f32[240,128]{1,0:T(8,128)S(1)} %pad_maximum_fusion.7), channel_id=1, source_target_pairs={{0,8},{8,0},{16,24},{24,16},{1,9},{9,1},{17,25},{25,17},{2,10},{10... | collective-permute-start | bytes 368648 | tf_op jit(solution)/shard_map/ppermute | solution.py:500

commit v2 on v1

--- a/solution.py
+++ b/solution.py
@@ -392,8 +392,13 @@
     cov_inverse[...], gram_inverse[...] = inverse_pair(both[0], both[1])
 
 
-def weight_kernel(realizations, sums, cov_inverse, offset, share, coeffs, mean, weights, pieces, rows):
-    count = coeffs.shape[0]
+def pair_kernel(coeffs, mean, pieces, rows):
+    fill_coeff_rows(coeffs[...] - mean[...], rows)
+    pieces[...] = stacked_halves(rows[...])
+
+
+def weight_kernel(realizations, sums, cov_inverse, offset, share, weights):
+    count = cov_inverse.shape[0]
     padded = weights.shape[1]
     pairs = pair_start(count // TILE)
     third = tiles_beside(sums[...], count) * (1.0 / realizations) - offset[...]
@@ -402,8 +407,6 @@
     lanes = lax.broadcasted_iota(jnp.int32, (count, padded), 1)
     unit = jnp.where(lanes - pairs == ids, 1.0, 0.0)
     weights[...] = stacked_halves(jnp.where(lanes < pairs, weight_map, unit))
-    fill_coeff_rows(coeffs[...] - mean[...], rows)
-    pieces[...] = stacked_halves(rows[...])
 
 
 def forcing_kernel(start, weights, extended, grad_x, grad_y, out, rows):
@@ -425,7 +428,8 @@
     lax.fori_loop(0, out.shape[0] // 2, body, 0)
 
 
-def ring_forcing_kernel(weights, extended, far_above, far_below, grad_y, ring, out_rows, out, edge_x, rows):
+def closing_kernel(weights, extended, far_above, far_below, grad_y, ring, *refs):
+    *moved, base, out_rows, edge_x, rows = refs
     count = weights.shape[0] // 2
     total = extended.shape[0]
     clear_rest(rows, count)
@@ -448,15 +452,14 @@
     lax.fori_loop(0, 2, body, 0)
     fill_pair_fields([ring.at[0], ring.at[1]], [(ring.at[2], ring.at[3])], rows)
     nonlinear = dot_halves(stack, rows[:, :LANES], NN)
-    out[...] = ring[4, count + 1 : count + 2, :] * (ring[4, 0:count, :] - TIME_STEP * nonlinear)
-
-
-def smooth_kernel(extended, moved, moved_ring, base):
-    total, count, _ = base.shape
-    beside = moved_ring[...]
-    for q in range(total):
+    beside = ring[4, count + 1 : count + 2, :] * (ring[4, 0:count, :] - TIME_STEP * nonlinear)
+    planes = [out_rows[0], out_rows[1]]
+    for piece in moved:
+        planes += [piece[q] for q in range(piece.shape[0])]
+    planes += [out_rows[2], out_rows[3]]
+    for q in range(base.shape[0]):
         water = extended[q + 4, count + 1 : count + 2, :]
-        base[q] = water * diffused(moved[q], moved[q + 2], moved[q + 4], beside, q)
+        base[q] = water * diffused(planes[q], planes[q + 2], planes[q + 4], beside, q)
 
 
 def finish_kernel(
@@ -472,8 +475,8 @@
     drift = jnp.dot(stack, pieces[0 : tens.shape[1], :], preferred_element_type=jnp.float32)
     drift += jnp.dot(stack, pieces[tens.shape[1] :, :], preferred_element_type=jnp.float32)
     drift = drift[:count] + drift[count:] - jnp.sum(tens * pair_cov[...], axis=1, keepdims=True)
-    solved = stacked_halves(dot32(projected, inverse, NN))
-    new_coeffs[...] = coeffs[...] - mean[...] + TIME_STEP * dot32(inverse, drift, NN)
+    solved = stacked_halves(dot_halves(stacked_halves(projected), inverse, NN))
+    new_coeffs[...] = coeffs[...] - mean[...] + TIME_STEP * dot_halves(stacked_halves(inverse), drift, NN)
     for x in range(total // 2):
         both = jnp.concatenate([shape[2 * x], shape[2 * x + 1]], axis=1)
         change = dot_halves(solved, both, NN)
@@ -547,6 +550,10 @@
 
 def shape32(*dims):
     return jax.ShapeDtypeStruct(dims, jnp.float32)
+
+
+def work(amount):
+    return pl.CostEstimate(flops=amount * 10**9, bytes_accessed=2**20, transcendentals=0)
 
 
 def vmem32(*dims):
@@ -679,49 +686,49 @@
     )(both)
     moments = joined(moments, other[0], lower_b)
     kept, moments, cov_inverse = tied(kept, moments, cov_inverse)
+    moments, late_coeffs = tied(moments, coeffs)
+    pieces = call(
+        pair_kernel,
+        out_shape=jax.ShapeDtypeStruct((2 * padded, rows_dev), jnp.bfloat16),
+        scratch_shapes=[vmem32(padded, rows_dev)],
+    )(late_coeffs, mean)
     sums = joined(moments, swap(moments, "row", row_a), lower_a)
-    kept, sums = tied(kept, sums)
-    weights, pieces = call(
-        functools.partial(weight_kernel, row_total),
-        out_shape=(
-            jax.ShapeDtypeStruct((2 * count, padded), jnp.bfloat16),
-            jax.ShapeDtypeStruct((2 * padded, rows_dev), jnp.bfloat16),
-        ),
-        scratch_shapes=[vmem32(padded, rows_dev)],
-    )(sums, cov_inverse, offset, share, coeffs, mean)
+    kept, pieces = tied(kept, pieces)
     col_bits = axis_bits("col")
     steps = later_steps("row") + [
         ("col", [i ^ (1 << bit) for i in range(lax.axis_size("col"))]) for bit in col_bits
     ]
 
-    def forcing(start, stop):
+    def forcing(weights, start, stop):
         return call(
             functools.partial(forcing_kernel, start),
+            cost_estimate=work(3),
             out_shape=shape32(2 * (stop - start), count, ny),
             scratch_shapes=[vmem32(padded, 2 * ny)],
         )(weights, extended, grad_x, grad_y)
 
-    def ring_forcing():
-        return call(
-            ring_forcing_kernel,
-            out_shape=(shape32(4, count, ny), shape32(count, ny)),
-            scratch_shapes=[vmem32(4, fields, ny), vmem32(padded, 2 * ny)],
-        )(weights, extended, far_above, far_below, grad_y, ring)
-
-    works = [functools.partial(forcing, 1 + nx * n // 2, 1 + nx * (n + 1) // 2) for n in range(2)] + [ring_forcing]
+    weights = None
     moved = []
-    for axis, partner in steps:
+    for number, (axis, partner) in enumerate(steps):
         total_kept = kept + swap(kept, axis, partner)
-        if works:
-            moved.append(works.pop(0)())
+        if number == 0:
+            kept, sums = tied(total_kept, sums)
+            continue
+        if weights is None:
+            weights = call(
+                functools.partial(weight_kernel, row_total),
+                cost_estimate=work(1),
+                out_shape=jax.ShapeDtypeStruct((2 * count, padded), jnp.bfloat16),
+            )(sums, cov_inverse, offset, share)
+        if number < 3:
+            moved.append(forcing(weights, 1 + nx * (number - 1) // 2, 1 + nx * number // 2))
         kept, weights, moved = tied(total_kept, weights, moved)
     kept = joined(kept, swap(kept, "row", row_b), lower_b)
-    while works:
-        moved.append(works.pop(0)())
-    moved_rows, moved_ring = moved.pop()
-    base = call(smooth_kernel, out_shape=shape32(2 * nx, count, ny))(
-        extended, jnp.concatenate([moved_rows[:2], *moved, moved_rows[2:]], axis=0), moved_ring
-    )
+    base = call(
+        closing_kernel,
+        out_shape=shape32(2 * nx, count, ny),
+        scratch_shapes=[vmem32(4, count, ny), vmem32(4, fields, ny), vmem32(padded, 2 * ny)],
+    )(weights, extended, far_above, far_below, grad_y, ring, *moved)
     kept, base = tied(kept, base)
     tensor = joined(kept, swap(kept, "row", row_a), lower_a)
 

time: 61.4 us -> 60.2 us (0.980)
  transfers between devices with their start and end apart: 13 -> 13, of which waited for: 11 -> 9; matrix products, arithmetic and copies ran while one was open for 0% -> 0% of each run, Pallas kernels for 36% -> 37%
where the time goes in v2:
time: 60.2 us; the launch traced here: 59.9 us
  Pallas kernels  25 us (42%)
  starting transfers between devices  18.2 us (30%)
  waiting for transfers between devices  12.7 us (21%)
  local copies, waits for them, and re-layouts  2.31 us (4%)
  between operations  1.14 us (2%)
    ppermute x13, starting transfers between devices, swap(): return lax.ppermute(values, axis, list(enumerate(partner)))  18.2 us
    ppermute x13, waiting for transfers between devices, swap(): return lax.ppermute(values, axis, list(enumerate(partner)))  12.7 us
    pallas_call x3, Pallas kernels, tensor_piece(): call(functools.partial(tensor_kernel, scale, start, stop), out_shape=shap...  6.01 us
    pallas_call x2, Pallas kernels, forcing(): call(functools.partial(forcing_kernel, start), cost_estimate=work(3), out...  5.33 us
    pallas_call x1, Pallas kernels, on_device(): call(inverse_kernel, out_shape=(shape32(count, count), shape32(count, cou...  4.07 us
    unnamed x19, local copies, waits for them, and re-layouts  2.29 us
    pallas_call x1, Pallas kernels, on_device(): call(closing_kernel, out_shape=shape32(2 * nx, count, ny), scratch_shapes...  2.18 us
    pallas_call x1, Pallas kernels, on_device(): call(finish_kernel, out_shape=(shape32(count * 2 * nx, ny), shape32(count...  1.68 us
  transfers between devices with their start and end apart: 13, of which 9 were waited for; matrix products, arithmetic and copies ran while one was open for 0% of the time, Pallas kernels for 37%

profile of v2, /device:TPU:0, one launch (start us, length us, event | category | flops | bytes accessed | tf_op | source)
XLA Modules:
  0.0 59.9 jit_solution(1305744969461497932)
XLA Ops:
  0.7 0.0 copy-start.6
  0.7 0.7 %copy-done.1 = s32[128,48]{0,1:T(8,128)S(1)} copy-done((s32[128,48]{0,1:T(8,128)S(1)}, s32[128,48]{0,1:T(8,128)}, u32[]{:S(2)}) %copy-start.1) | copy-done | bytes 24600
  1.4 0.0 copy-done.6
  1.4 1.0 %copy-done = f32[48,2,8,128]{3,2,1,0:T(8,128)S(1)} copy-done((f32[48,2,8,128]{3,2,1,0:T(8,128)S(1)}, f32[48,2,8,128]{3,2,1,0:T(8,128)}, u32[]{:S(2)}) %copy-start) | copy-done | bytes 393240
  2.4 1.2 %shard_map.95 = (f32[24,56,128]{2,1,0:T(8,128)S(1)}, f32[480,128]{1,0:T(8,128)S(1)}, f32[24,128]{1,0:T(8,128)S(1)}, f32[48,128]{1,0:T(8,128)S(1)}) custom-call(f32[768,128]{1,0:T(8,128)S(1)} %bitcast.15, f32[16,128]{1,0:T(8,128)S(1)} %bitcast.21, s32[8,128]{1,0:T(8,128)S(1)} %copy-done.6, s32[48,128]{1,0:T(8,128)S(1)} %bitcast.20, ...), custom_call_target="tpu_custom_call" | custom-call | tf_op jit(solution)/shard_map/pallas_call | solution.py:583
  3.7 0.5 collective-permute-start
  4.2 0.8 %shard_map.96 = (f32[16,56,128]{2,1,0:T(8,128)S(1)}, f32[16,56,128]{2,1,0:T(8,128)S(1)}, f32[56,128]{1,0:T(8,128)S(1)}, f32[56,128]{1,0:T(8,128)S(1)}) custom-call(f32[24,56,128]{2,1,0:T(8,128)S(1)} %get-tuple-element.71.planes), custom_call_target="tpu_custom_call" | custom-call | tf_op jit(solution)/shard_map/pallas_call | solution.py:595
  5.0 0.4 collective-permute-done
  5.5 2.7 %collective-permute-start.1 = (f32[256,128]{1,0:T(8,128)S(1)}, f32[256,128]{1,0:T(8,128)S(1)}, u32[]{:S(2)}, u32[]{:S(2)}) collective-permute-start(f32[256,128]{1,0:T(8,128)S(1)} %pad_maximum_fusion.3), channel_id=1, source_target_pairs={{0,24},{8,16},{16,8},{24,0},{1,25},{9,17},{17,9},{25,1},{2,26},{10... | collective-permute-start | bytes 393224 | tf_op jit(solution)/shard_map/ppermute | solution.py:503
  8.2 1.5 %shard_map.97.refs_0_ = f32[480,128]{1,0:T(8,128)S(1)} custom-call(f32[24,56,128]{2,1,0:T(8,128)S(1)} %get-tuple-element.71.planes, f32[16,56,128]{2,1,0:T(8,128)S(1)} %get-tuple-element.77.grad_x, f32[16,56,128]{2,1,0:T(8,128)S(1)} %get-tuple-element.78.grad_y), custom_call_target="tpu_custom_call" | custom-call | tf_op jit(solution)/shard_map/pallas_call | solution.py:604
  9.8 2.1 %collective-permute-done.1 = f32[256,128]{1,0:T(8,128)S(1)} collective-permute-done((f32[256,128]{1,0:T(8,128)S(1)}, f32[256,128]{1,0:T(8,128)S(1)}, u32[]{:S(2)}, u32[]{:S(2)}) %collective-permute-start.1) | collective-permute-done | bytes 131104 | tf_op jit(solution)/shard_map/ppermute | solution.py:503
  11.9 0.2 shard_map.98
  12.1 2.2 %collective-permute-start.2 = (f32[200,128]{1,0:T(8,128)S(1)}, f32[200,128]{1,0:T(8,128)S(1)}, u32[]{:S(2)}, u32[]{:S(2)}) collective-permute-start(f32[200,128]{1,0:T(8,128)S(1)} %pad_maximum_fusion.7), channel_id=1, source_target_pairs={{0,1},{1,0},{2,3},{3,2},{4,5},{5,4},{6,7},{7,6},{8,9},{9,8},{10,11... | collective-permute-start | bytes 307208 | tf_op jit(solution)/shard_map/ppermute | solution.py:503
  14.3 2.2 %shard_map.99.refs_0_ = f32[480,128]{1,0:T(8,128)S(1)} custom-call(f32[24,56,128]{2,1,0:T(8,128)S(1)} %get-tuple-element.71.planes, f32[16,56,128]{2,1,0:T(8,128)S(1)} %get-tuple-element.77.grad_x, f32[16,56,128]{2,1,0:T(8,128)S(1)} %get-tuple-element.78.grad_y, f32[480,128]{1,0:T(8,128)S(1)} %shard_map.97.refs_0_), custom_call_target="tpu_custom_call" | custom-call | tf_op jit(solution)/shard_map/pallas_call | solution.py:604
  16.5 0.9 %collective-permute-done.2 = f32[200,128]{1,0:T(8,128)S(1)} collective-permute-done((f32[200,128]{1,0:T(8,128)S(1)}, f32[200,128]{1,0:T(8,128)S(1)}, u32[]{:S(2)}, u32[]{:S(2)}) %collective-permute-start.2) | collective-permute-done | bytes 102432 | tf_op jit(solution)/shard_map/ppermute | solution.py:503
  17.5 4.8 %collective-permute-start.3 = (f32[200,128]{1,0:T(8,128)S(1)}, f32[200,128]{1,0:T(8,128)S(1)}, u32[]{:S(2)}, u32[]{:S(2)}) collective-permute-start(f32[200,128]{1,0:T(8,128)S(1)} %pad_maximum_fusion.8), channel_id=1, source_target_pairs={{0,7},{1,2},{2,1},{3,4},{4,3},{5,6},{6,5},{7,0},{8,15},{9,10},{10,... | collective-permute-start | bytes 307208 | tf_op jit(solution)/shard_map/ppermute | solution.py:503
  22.3 2.3 %shard_map.100.before = f32[480,128]{1,0:T(8,128)S(1)} custom-call(f32[24,56,128]{2,1,0:T(8,128)S(1)} %get-tuple-element.71.planes, f32[16,56,128]{2,1,0:T(8,128)S(1)} %get-tuple-element.77.grad_x, f32[16,56,128]{2,1,0:T(8,128)S(1)} %get-tuple-element.78.grad_y, f32[480,128]{1,0:T(8,128)S(1)} %shard_map.99.refs_0_), custom_call_target="tpu_custom_call" | custom-call | tf_op jit(solution)/shard_map/pallas_call | solution.py:604
  24.6 0.4 collective-permute-done.3
  25.0 1.0 %collective-permute-start.4 = (f32[144,128]{1,0:T(8,128)S(1)}, f32[144,128]{1,0:T(8,128)S(1)}, u32[]{:S(2)}, u32[]{:S(2)}) collective-permute-start(f32[144,128]{1,0:T(8,128)S(1)} %pad_maximum_fusion.9), channel_id=1, source_target_pairs={{0,4},{1,5},{2,6},{3,7},{4,0},{5,1},{6,2},{7,3},{8,12},{9,13},{10,... | collective-permute-start | bytes 221192 | tf_op jit(solution)/shard_map/ppermute | solution.py:503
  26.1 1.2 %shard_map.102 = (f32[20,56,128]{2,1,0:T(8,128)S(1)}, f32[20,56,128]{2,1,0:T(8,128)S(1)}, f32[5,56,128]{2,1,0:T(8,128)S(1)}, f32[16,48,128]{2,1,0:T(8,128)S(1)}) custom-call(f32[24,56,128]{2,1,0:T(8,128)S(1)} %get-tuple-element.93.extended, f32[56,128]{1,0:T(8,128)S(1)} %get-tuple-element.94.left, f32[56,128]{1,0:T(8,128)S(1)} %get-tuple-element.95.right, ...), custom_call_target="tpu_custom_call" | custom-call | tf_op jit(solution)/shard_map/pallas_call | solution.py:661
  27.2 1.3 %shard_map.101 = f32[480,128]{1,0:T(8,128)S(1)} custom-call(f32[24,56,128]{2,1,0:T(8,128)S(1)} %get-tuple-element.93.extended, f32[56,128]{1,0:T(8,128)S(1)} %get-tuple-element.94.left, f32[56,128]{1,0:T(8,128)S(1)} %get-tuple-element.95.right, f32[56,128]{1,0:T(8,128)S(1)} %get-tuple-element.86.col_first, f32[56,128]{1,0:T(8,128)S(1)} %get-tuple-element.85.col_last, ...), custom_call_target="tpu_custom_call" | custom-call | tf_op jit(solution)/shard_map/pallas_call | solution.py:656
  28.6 2.0 %collective-permute-done.4 = f32[144,128]{1,0:T(8,128)S(1)} collective-permute-done((f32[144,128]{1,0:T(8,128)S(1)}, f32[144,128]{1,0:T(8,128)S(1)}, u32[]{:S(2)}, u32[]{:S(2)}) %collective-permute-start.4) | collective-permute-done | bytes 73760 | tf_op jit(solution)/shard_map/ppermute | solution.py:503
  30.6 0.0 copy-start.2
  30.6 0.0 copy-start.4
  30.6 0.0 copy-start.5
  30.6 0.1 collective-permute-start.5
  30.7 0.6 copy-done.2
  31.3 0.0 copy-done.4
  31.3 0.0 copy-done.5
  31.3 0.7 %shard_map.103 = (f32[2,48,48]{2,1,0:T(8,128)S(1)}, f32[48,128]{1,0:T(8,128)S(1)}, f32[1,1280]{1,0:T(1,128)S(1)}, f32[48,1280]{1,0:T(8,128)S(1)}) custom-call(f32[24,128]{1,0:T(8,128)S(1)} %slice_add_fusion.7.early, s32[1,1280]{1,0:T(1,128)S(1)} %copy-done.5, s32[1,1280]{1,0:T(1,128)S(1)} %copy-done.4, f32[1,1280]{1,0:T(1,128)S(1)} %copy-done.2), custom_call_target="tpu_custom_call" | custom-call | tf_op jit(solution)/shard_map/pallas_call | solution.py:674
  32.0 0.1 collective-permute-done.5
  32.2 1.3 %collective-permute-start.6 = (f32[240,128]{1,0:T(8,128)S(1)}, f32[240,128]{1,0:T(8,128)S(1)}, u32[]{:S(2)}, u32[]{:S(2)}) collective-permute-start(f32[240,128]{1,0:T(8,128)S(1)} %pad_maximum_fusion.4), channel_id=1, source_target_pairs={{0,24},{8,16},{16,8},{24,0},{1,25},{9,17},{17,9},{25,1},{2,26},{10... | collective-permute-start | bytes 368648 | tf_op jit(solution)/shard_map/ppermute | solution.py:503
  33.5 4.1 %shard_map.104 = (f32[48,48]{1,0:T(8,128)S(1)}, f32[48,48]{1,0:T(8,128)S(1)}) custom-call(f32[2,48,48]{2,1,0:T(8,128)S(1)} %get-tuple-element.104.both), custom_call_target="tpu_custom_call" | custom-call | tf_op jit(solution)/shard_map/pallas_call | solution.py:684
  37.7 0.4 collective-permute-start.8
  38.1 0.1 shard_map.105.pieces
  38.2 0.5 collective-permute-start.7
  38.7 3.8 %collective-permute-done.7 = f32[120,128]{1,0:T(8,128)S(1)} collective-permute-done((f32[120,128]{1,0:T(8,128)S(1)}, f32[120,128]{1,0:T(8,128)S(1)}, u32[]{:S(2)}, u32[]{:S(2)}) %collective-permute-start.7) | collective-permute-done | bytes 61472 | tf_op jit(solution)/shard_map/ppermute | solution.py:503
  42.6 1.3 %collective-permute-start.9 = (f32[120,128]{1,0:T(8,128)S(1)}, f32[120,128]{1,0:T(8,128)S(1)}, u32[]{:S(2)}, u32[]{:S(2)}) collective-permute-start(f32[120,128]{1,0:T(8,128)S(1)} %add.113), channel_id=1, source_target_pairs={{0,2},{1,3},{2,0},{3,1},{4,6},{5,7},{6,4},{7,5},{8,10},{9,11},{10,... | collective-permute-start | bytes 184328 | tf_op jit(solution)/shard_map/ppermute | solution.py:503
  43.9 0.3 shard_map.106.weights
  44.2 2.7 %shard_map.107.refs_0_ = f32[8,48,128]{2,1,0:T(8,128)S(1)} custom-call(bf16[96,1280]{1,0:T(8,128)(2,1)S(1)} %shard_map.106.weights, f32[24,56,128]{2,1,0:T(8,128)S(1)} %get-tuple-element.93.extended, f32[20,56,128]{2,1,0:T(8,128)S(1)} %get-tuple-element.117.grad_x, f32[20,56,128]{2,1,0:T(8,128)S(1)} %get-tuple-element.118.grad_y), custom_call_target="tpu_custom_call" | custom-call | flops 3000000000 | bytes 1048576 | tf_op jit(solution)/shard_map/pallas_call | solution.py:703
  46.9 2.8 %collective-permute-start.10 = (f32[120,128]{1,0:T(8,128)S(1)}, f32[120,128]{1,0:T(8,128)S(1)}, u32[]{:S(2)}, u32[]{:S(2)}) collective-permute-start(f32[120,128]{1,0:T(8,128)S(1)} %add.114), channel_id=1, source_target_pairs={{0,4},{1,5},{2,6},{3,7},{4,0},{5,1},{6,2},{7,3},{8,12},{9,13},{10,... | collective-permute-start | bytes 184328 | tf_op jit(solution)/shard_map/ppermute | solution.py:503
  49.7 2.7 %shard_map.108.refs_1_ = f32[8,48,128]{2,1,0:T(8,128)S(1)} custom-call(bf16[96,1280]{1,0:T(8,128)(2,1)S(1)} %shard_map.106.weights, f32[24,56,128]{2,1,0:T(8,128)S(1)} %get-tuple-element.93.extended, f32[20,56,128]{2,1,0:T(8,128)S(1)} %get-tuple-element.117.grad_x, f32[20,56,128]{2,1,0:T(8,128)S(1)} %get-tuple-element.118.grad_y), custom_call_target="tpu_custom_call" | custom-call | flops 3000000000 | bytes 1048576 | tf_op jit(solution)/shard_map/pallas_call | solution.py:703
  52.4 0.4 collective-permute-start.11
  52.8 2.2 %shard_map.109.base = f32[16,48,128]{2,1,0:T(8,128)S(1)} custom-call(bf16[96,1280]{1,0:T(8,128)(2,1)S(1)} %shard_map.106.weights, f32[24,56,128]{2,1,0:T(8,128)S(1)} %get-tuple-element.93.extended, f32[2,56,128]{2,1,0:T(8,128)S(1)} %bitcast.17, f32[2,56,128]{2,1,0:T(8,128)S(1)} %bitcast.16, f32[20,56,128]{2,1,0:T(8,128)S(1)} %get-tuple-element.118.grad_y, ...), custom_call_target="tpu_custom_call" | custom-call | tf_op jit(solution)/shard_map/pallas_call | solution.py:727
  55.0 1.8 %collective-permute-done.11 = f32[120,128]{1,0:T(8,128)S(1)} collective-permute-done((f32[120,128]{1,0:T(8,128)S(1)}, f32[120,128]{1,0:T(8,128)S(1)}, u32[]{:S(2)}, u32[]{:S(2)}) %collective-permute-start.11) | collective-permute-done | bytes 61472 | tf_op jit(solution)/shard_map/ppermute | solution.py:503
  56.8 0.2 collective-permute-start.12
  57.0 1.2 %collective-permute-done.12 = f32[240,128]{1,0:T(8,128)S(1)} collective-permute-done((f32[240,128]{1,0:T(8,128)S(1)}, f32[240,128]{1,0:T(8,128)S(1)}, u32[]{:S(2)}, u32[]{:S(2)}) %collective-permute-start.12) | collective-permute-done | bytes 122912 | tf_op jit(solution)/shard_map/ppermute | solution.py:503
  58.2 1.7 %shard_map.110 = (f32[768,128]{1,0:T(8,128)}, f32[48,128]{1,0:T(8,128)}) custom-call(f32[480,128]{1,0:T(8,128)S(1)} %pad_maximum_fusion.1.tensor, bf16[96,1280]{1,0:T(8,128)(2,1)S(1)} %shard_map.106.weights, bf16[2560,128]{1,0:T(8,128)(2,1)S(1)} %shard_map.105.pieces, f32[48,48]{1,0:T(8,128)S(1)} %get-tuple-element.130.gram_inverse, ...), custom_call_target="tpu_custom_call" | custom-call | tf_op jit(solution)/shard_map/pallas_call | solution.py:735
  (54 shorter events, 0.6 us)
Async XLA Ops:
  0.6 0.7 %copy-start.1 = (s32[128,48]{0,1:T(8,128)S(1)}, s32[128,48]{0,1:T(8,128)}, u32[]{:S(2)}) copy-start(s32[128,48]{0,1:T(8,128)} %param.10) | copy-start | bytes 73732
  0.7 0.7 %copy-start.3 = (f32[2,8,128]{2,1,0:T(8,128)S(1)}, f32[2,8,128]{2,1,0:T(8,128)}, u32[]{:S(2)}) copy-start(f32[2,8,128]{2,1,0:T(8,128)} %param.9) | copy-start | bytes 24580
  0.7 0.7 %copy-start.6 = (s32[8,128]{1,0:T(8,128)S(1)}, s32[8,128]{1,0:T(8,128)}, u32[]{:S(2)}) copy-start(s32[8,128]{1,0:T(8,128)} %water.1) | copy-start | bytes 12292
  0.7 0.7 %copy-start.7 = (f32[48]{0:T(128)S(1)}, f32[48]{0:T(128)}, u32[]{:S(2)}) copy-start(f32[48]{0:T(128)} %param.11) | copy-start | bytes 580
  1.4 1.0 %copy-start = (f32[48,2,8,128]{3,2,1,0:T(8,128)S(1)}, f32[48,2,8,128]{3,2,1,0:T(8,128)}, u32[]{:S(2)}) copy-start(f32[48,2,8,128]{3,2,1,0:T(8,128)} %param.8) | copy-start | bytes 1179652
  3.7 1.7 %collective-permute-start = (f32[600,128]{1,0:T(8,128)S(1)}, f32[600,128]{1,0:T(8,128)S(1)}, u32[]{:S(2)}, u32[]{:S(2)}) collective-permute-start(f32[600,128]{1,0:T(8,128)S(1)} %constant_dynamic-update-slice_fusion), channel_id=1, source_target_pairs={{0,8},{8,0},{16,24},{24,16},{1,9},{9,1},{17,25},{25,17},{2,10},{10... | collective-permute-start | bytes 921608 | tf_op jit(solution)/shard_map/ppermute | solution.py:503
  5.5 6.3 %collective-permute-start.1 = (f32[256,128]{1,0:T(8,128)S(1)}, f32[256,128]{1,0:T(8,128)S(1)}, u32[]{:S(2)}, u32[]{:S(2)}) collective-permute-start(f32[256,128]{1,0:T(8,128)S(1)} %pad_maximum_fusion.3), channel_id=1, source_target_pairs={{0,24},{8,16},{16,8},{24,0},{1,25},{9,17},{17,9},{25,1},{2,26},{10... | collective-permute-start | bytes 393224 | tf_op jit(solution)/shard_map/ppermute | solution.py:503
  12.1 5.4 %collective-permute-start.2 = (f32[200,128]{1,0:T(8,128)S(1)}, f32[200,128]{1,0:T(8,128)S(1)}, u32[]{:S(2)}, u32[]{:S(2)}) collective-permute-start(f32[200,128]{1,0:T(8,128)S(1)} %pad_maximum_fusion.7), channel_id=1, source_target_pairs={{0,1},{1,0},{2,3},{3,2},{4,5},{5,4},{6,7},{7,6},{8,9},{9,8},{10,11... | collective-permute-start | bytes 307208 | tf_op jit(solution)/shard_map/ppermute | solution.py:503
  17.5 7.5 %collective-permute-start.3 = (f32[200,128]{1,0:T(8,128)S(1)}, f32[200,128]{1,0:T(8,128)S(1)}, u32[]{:S(2)}, u32[]{:S(2)}) collective-permute-start(f32[200,128]{1,0:T(8,128)S(1)} %pad_maximum_fusion.8), channel_id=1, source_target_pairs={{0,7},{1,2},{2,1},{3,4},{4,3},{5,6},{6,5},{7,0},{8,15},{9,10},{10,... | collective-permute-start | bytes 307208 | tf_op jit(solution)/shard_map/ppermute | solution.py:503
  25.0 5.5 %collective-permute-start.4 = (f32[144,128]{1,0:T(8,128)S(1)}, f32[144,128]{1,0:T(8,128)S(1)}, u32[]{:S(2)}, u32[]{:S(2)}) collective-permute-start(f32[144,128]{1,0:T(8,128)S(1)} %pad_maximum_fusion.9), channel_id=1, source_target_pairs={{0,4},{1,5},{2,6},{3,7},{4,0},{5,1},{6,2},{7,3},{8,12},{9,13},{10,... | collective-permute-start | bytes 221192 | tf_op jit(solution)/shard_map/ppermute | solution.py:503
  30.6 0.7 %copy-start.2 = (f32[1,1280]{1,0:T(1,128)S(1)}, f32[1,1280]{1,0:T(1,128)}, u32[]{:S(2)}) copy-start(f32[1,1280]{1,0:T(1,128)} %constant.73.clone.share) | copy-start | bytes 15364
  30.6 0.7 %copy-start.4 = (s32[1,1280]{1,0:T(1,128)S(1)}, s32[1,1280]{1,0:T(1,128)}, u32[]{:S(2)}) copy-start(s32[1,1280]{1,0:T(1,128)} %constant.72.clone.second) | copy-start | bytes 15364
  30.6 0.7 %copy-start.5 = (s32[1,1280]{1,0:T(1,128)S(1)}, s32[1,1280]{1,0:T(1,128)}, u32[]{:S(2)}) copy-start(s32[1,1280]{1,0:T(1,128)} %constant.71.clone.first) | copy-start | bytes 15364
  30.6 1.5 %collective-permute-start.5 = (f32[352,128]{1,0:T(8,128)S(1)}, f32[352,128]{1,0:T(8,128)S(1)}, u32[]{:S(2)}, u32[]{:S(2)}) collective-permute-start(f32[352,128]{1,0:T(8,128)S(1)} %pad_maximum_fusion.2), channel_id=1, source_target_pairs={{0,8},{8,0},{16,24},{24,16},{1,9},{9,1},{17,25},{25,17},{2,10},{10... | collective-permute-start | bytes 540680 | tf_op jit(solution)/shard_map/ppermute | solution.py:503
  32.2 5.4 %collective-permute-start.6 = (f32[240,128]{1,0:T(8,128)S(1)}, f32[240,128]{1,0:T(8,128)S(1)}, u32[]{:S(2)}, u32[]{:S(2)}) collective-permute-start(f32[240,128]{1,0:T(8,128)S(1)} %pad_maximum_fusion.4), channel_id=1, source_target_pairs={{0,24},{8,16},{16,8},{24,0},{1,25},{9,17},{17,9},{25,1},{2,26},{10... | collective-permute-start | bytes 368648 | tf_op jit(solution)/shard_map/ppermute | solution.py:503
  37.7 4.9 %collective-permute-start.8 = (f32[240,128]{1,0:T(8,128)S(1)}, f32[240,128]{1,0:T(8,128)S(1)}, u32[]{:S(2)}, u32[]{:S(2)}) collective-permute-start(f32[240,128]{1,0:T(8,128)S(1)} %pad_maximum_fusion.5), channel_id=1, source_target_pairs={{0,8},{8,0},{16,24},{24,16},{1,9},{9,1},{17,25},{25,17},{2,10},{10... | collective-permute-start | bytes 368648 | tf_op jit(solution)/shard_map/ppermute | solution.py:503
  38.2 4.3 %collective-permute-start.7 = (f32[120,128]{1,0:T(8,128)S(1)}, f32[120,128]{1,0:T(8,128)S(1)}, u32[]{:S(2)}, u32[]{:S(2)}) collective-permute-start(f32[120,128]{1,0:T(8,128)S(1)} %get-tuple-element.111), channel_id=1, source_target_pairs={{0,1},{1,0},{2,3},{3,2},{4,5},{5,4},{6,7},{7,6},{8,9},{9,8},{10,11... | collective-permute-start | bytes 184328 | tf_op jit(solution)/shard_map/ppermute | solution.py:503
  42.6 4.3 %collective-permute-start.9 = (f32[120,128]{1,0:T(8,128)S(1)}, f32[120,128]{1,0:T(8,128)S(1)}, u32[]{:S(2)}, u32[]{:S(2)}) collective-permute-start(f32[120,128]{1,0:T(8,128)S(1)} %add.113), channel_id=1, source_target_pairs={{0,2},{1,3},{2,0},{3,1},{4,6},{5,7},{6,4},{7,5},{8,10},{9,11},{10,... | collective-permute-start | bytes 184328 | tf_op jit(solution)/shard_map/ppermute | solution.py:503
  46.9 5.5 %collective-permute-start.10 = (f32[120,128]{1,0:T(8,128)S(1)}, f32[120,128]{1,0:T(8,128)S(1)}, u32[]{:S(2)}, u32[]{:S(2)}) collective-permute-start(f32[120,128]{1,0:T(8,128)S(1)} %add.114), channel_id=1, source_target_pairs={{0,4},{1,5},{2,6},{3,7},{4,0},{5,1},{6,2},{7,3},{8,12},{9,13},{10,... | collective-permute-start | bytes 184328 | tf_op jit(solution)/shard_map/ppermute | solution.py:503
  52.4 4.3 %collective-permute-start.11 = (f32[120,128]{1,0:T(8,128)S(1)}, f32[120,128]{1,0:T(8,128)S(1)}, u32[]{:S(2)}, u32[]{:S(2)}) collective-permute-start(f32[120,128]{1,0:T(8,128)S(1)} %add.115), channel_id=1, source_target_pairs={{0,24},{8,16},{16,8},{24,0},{1,25},{9,17},{17,9},{25,1},{2,26},{10... | collective-permute-start | bytes 184328 | tf_op jit(solution)/shard_map/ppermute | solution.py:503
  56.8 1.4 %collective-permute-start.12 = (f32[240,128]{1,0:T(8,128)S(1)}, f32[240,128]{1,0:T(8,128)S(1)}, u32[]{:S(2)}, u32[]{:S(2)}) collective-permute-start(f32[240,128]{1,0:T(8,128)S(1)} %pad_maximum_fusion.6), channel_id=1, source_target_pairs={{0,8},{8,0},{16,24},{24,16},{1,9},{9,1},{17,25},{25,17},{2,10},{10... | collective-permute-start | bytes 368648 | tf_op jit(solution)/shard_map/ppermute | solution.py:503

commit v3 on v2

--- a/solution.py
+++ b/solution.py
@@ -696,7 +696,7 @@
     kept, pieces = tied(kept, pieces)
     col_bits = axis_bits("col")
     steps = later_steps("row") + [
-        ("col", [i ^ (1 << bit) for i in range(lax.axis_size("col"))]) for bit in col_bits
+        ("col", [i ^ (1 << bit) for i in range(lax.axis_size("col"))]) for bit in col_bits[:1] + col_bits[:0:-1]
     ]
 
     def forcing(weights, start, stop):

time: 60.2 us -> 59.9 us (level)
  starting transfers between devices: 18.2 us -> 17.3 us
    ppermute x13, starting transfers between devices: 18.2 us -> 17.3 us  [swap(): return lax.ppermute(values, axis, list(enumerate(partner)))]
  transfers between devices with their start and end apart: 13 -> 13, of which waited for: 9 -> 10; matrix products, arithmetic and copies ran while one was open for 0% -> 0% of each run, Pallas kernels for 37% -> 37%
where the time goes in v3:
time: 59.9 us; the launch traced here: 59.6 us
  Pallas kernels  25 us (42%)
  starting transfers between devices  17.3 us (29%)
  waiting for transfers between devices  13.3 us (22%)
  local copies, waits for them, and re-layouts  2.31 us (4%)
  between operations  1.13 us (2%)
    ppermute x13, starting transfers between devices, swap(): return lax.ppermute(values, axis, list(enumerate(partner)))  17.3 us
    ppermute x13, waiting for transfers between devices, swap(): return lax.ppermute(values, axis, list(enumerate(partner)))  13.3 us
    pallas_call x3, Pallas kernels, tensor_piece(): call(functools.partial(tensor_kernel, scale, start, stop), out_shape=shap...  6.01 us
    pallas_call x2, Pallas kernels, forcing(): call(functools.partial(forcing_kernel, start), cost_estimate=work(3), out...  5.33 us
    pallas_call x1, Pallas kernels, on_device(): call(inverse_kernel, out_shape=(shape32(count, count), shape32(count, cou...  4.07 us
    unnamed x19, local copies, waits for them, and re-layouts  2.29 us
    pallas_call x1, Pallas kernels, on_device(): call(closing_kernel, out_shape=shape32(2 * nx, count, ny), scratch_shapes...  2.18 us
    pallas_call x1, Pallas kernels, on_device(): call(finish_kernel, out_shape=(shape32(count * 2 * nx, ny), shape32(count...  1.67 us
  transfers between devices with their start and end apart: 13, of which 10 were waited for; matrix products, arithmetic and copies ran while one was open for 0% of the time, Pallas kernels for 37%

profile of v3, /device:TPU:0, one launch (start us, length us, event | category | flops | bytes accessed | tf_op | source)
XLA Modules:
  0.0 59.6 jit_solution(13902521851609768409)
XLA Ops:
  0.7 0.7 %copy-done.1 = s32[128,48]{0,1:T(8,128)S(1)} copy-done((s32[128,48]{0,1:T(8,128)S(1)}, s32[128,48]{0,1:T(8,128)}, u32[]{:S(2)}) %copy-start.1) | copy-done | bytes 24600
  1.4 0.0 copy-done.6
  1.4 1.0 %copy-done = f32[48,2,8,128]{3,2,1,0:T(8,128)S(1)} copy-done((f32[48,2,8,128]{3,2,1,0:T(8,128)S(1)}, f32[48,2,8,128]{3,2,1,0:T(8,128)}, u32[]{:S(2)}) %copy-start) | copy-done | bytes 393240
  2.4 1.2 %shard_map.95 = (f32[24,56,128]{2,1,0:T(8,128)S(1)}, f32[480,128]{1,0:T(8,128)S(1)}, f32[24,128]{1,0:T(8,128)S(1)}, f32[48,128]{1,0:T(8,128)S(1)}) custom-call(f32[768,128]{1,0:T(8,128)S(1)} %bitcast.15, f32[16,128]{1,0:T(8,128)S(1)} %bitcast.21, s32[8,128]{1,0:T(8,128)S(1)} %copy-done.6, s32[48,128]{1,0:T(8,128)S(1)} %bitcast.20, ...), custom_call_target="tpu_custom_call" | custom-call | tf_op jit(solution)/shard_map/pallas_call | solution.py:583
  3.7 0.5 collective-permute-start
  4.2 0.8 %shard_map.96 = (f32[16,56,128]{2,1,0:T(8,128)S(1)}, f32[16,56,128]{2,1,0:T(8,128)S(1)}, f32[56,128]{1,0:T(8,128)S(1)}, f32[56,128]{1,0:T(8,128)S(1)}) custom-call(f32[24,56,128]{2,1,0:T(8,128)S(1)} %get-tuple-element.71.planes), custom_call_target="tpu_custom_call" | custom-call | tf_op jit(solution)/shard_map/pallas_call | solution.py:595
  5.0 0.4 collective-permute-done
  5.5 2.7 %collective-permute-start.1 = (f32[256,128]{1,0:T(8,128)S(1)}, f32[256,128]{1,0:T(8,128)S(1)}, u32[]{:S(2)}, u32[]{:S(2)}) collective-permute-start(f32[256,128]{1,0:T(8,128)S(1)} %pad_maximum_fusion.3), channel_id=1, source_target_pairs={{0,24},{8,16},{16,8},{24,0},{1,25},{9,17},{17,9},{25,1},{2,26},{10... | collective-permute-start | bytes 393224 | tf_op jit(solution)/shard_map/ppermute | solution.py:503
  8.2 1.5 %shard_map.97.refs_0_ = f32[480,128]{1,0:T(8,128)S(1)} custom-call(f32[24,56,128]{2,1,0:T(8,128)S(1)} %get-tuple-element.71.planes, f32[16,56,128]{2,1,0:T(8,128)S(1)} %get-tuple-element.77.grad_x, f32[16,56,128]{2,1,0:T(8,128)S(1)} %get-tuple-element.78.grad_y), custom_call_target="tpu_custom_call" | custom-call | tf_op jit(solution)/shard_map/pallas_call | solution.py:604
  9.8 2.1 %collective-permute-done.1 = f32[256,128]{1,0:T(8,128)S(1)} collective-permute-done((f32[256,128]{1,0:T(8,128)S(1)}, f32[256,128]{1,0:T(8,128)S(1)}, u32[]{:S(2)}, u32[]{:S(2)}) %collective-permute-start.1) | collective-permute-done | bytes 131104 | tf_op jit(solution)/shard_map/ppermute | solution.py:503
  11.9 0.2 shard_map.98
  12.1 2.2 %collective-permute-start.2 = (f32[200,128]{1,0:T(8,128)S(1)}, f32[200,128]{1,0:T(8,128)S(1)}, u32[]{:S(2)}, u32[]{:S(2)}) collective-permute-start(f32[200,128]{1,0:T(8,128)S(1)} %pad_maximum_fusion.7), channel_id=1, source_target_pairs={{0,1},{1,0},{2,3},{3,2},{4,5},{5,4},{6,7},{7,6},{8,9},{9,8},{10,11... | collective-permute-start | bytes 307208 | tf_op jit(solution)/shard_map/ppermute | solution.py:503
  14.3 2.2 %shard_map.99.refs_0_ = f32[480,128]{1,0:T(8,128)S(1)} custom-call(f32[24,56,128]{2,1,0:T(8,128)S(1)} %get-tuple-element.71.planes, f32[16,56,128]{2,1,0:T(8,128)S(1)} %get-tuple-element.77.grad_x, f32[16,56,128]{2,1,0:T(8,128)S(1)} %get-tuple-element.78.grad_y, f32[480,128]{1,0:T(8,128)S(1)} %shard_map.97.refs_0_), custom_call_target="tpu_custom_call" | custom-call | tf_op jit(solution)/shard_map/pallas_call | solution.py:604
  16.5 0.9 %collective-permute-done.2 = f32[200,128]{1,0:T(8,128)S(1)} collective-permute-done((f32[200,128]{1,0:T(8,128)S(1)}, f32[200,128]{1,0:T(8,128)S(1)}, u32[]{:S(2)}, u32[]{:S(2)}) %collective-permute-start.2) | collective-permute-done | bytes 102432 | tf_op jit(solution)/shard_map/ppermute | solution.py:503
  17.5 4.8 %collective-permute-start.3 = (f32[200,128]{1,0:T(8,128)S(1)}, f32[200,128]{1,0:T(8,128)S(1)}, u32[]{:S(2)}, u32[]{:S(2)}) collective-permute-start(f32[200,128]{1,0:T(8,128)S(1)} %pad_maximum_fusion.8), channel_id=1, source_target_pairs={{0,7},{1,2},{2,1},{3,4},{4,3},{5,6},{6,5},{7,0},{8,15},{9,10},{10,... | collective-permute-start | bytes 307208 | tf_op jit(solution)/shard_map/ppermute | solution.py:503
  22.3 2.3 %shard_map.100.before = f32[480,128]{1,0:T(8,128)S(1)} custom-call(f32[24,56,128]{2,1,0:T(8,128)S(1)} %get-tuple-element.71.planes, f32[16,56,128]{2,1,0:T(8,128)S(1)} %get-tuple-element.77.grad_x, f32[16,56,128]{2,1,0:T(8,128)S(1)} %get-tuple-element.78.grad_y, f32[480,128]{1,0:T(8,128)S(1)} %shard_map.99.refs_0_), custom_call_target="tpu_custom_call" | custom-call | tf_op jit(solution)/shard_map/pallas_call | solution.py:604
  24.6 0.4 collective-permute-done.3
  25.0 1.0 %collective-permute-start.4 = (f32[144,128]{1,0:T(8,128)S(1)}, f32[144,128]{1,0:T(8,128)S(1)}, u32[]{:S(2)}, u32[]{:S(2)}) collective-permute-start(f32[144,128]{1,0:T(8,128)S(1)} %pad_maximum_fusion.9), channel_id=1, source_target_pairs={{0,4},{1,5},{2,6},{3,7},{4,0},{5,1},{6,2},{7,3},{8,12},{9,13},{10,... | collective-permute-start | bytes 221192 | tf_op jit(solution)/shard_map/ppermute | solution.py:503
  26.1 1.2 %shard_map.102 = (f32[20,56,128]{2,1,0:T(8,128)S(1)}, f32[20,56,128]{2,1,0:T(8,128)S(1)}, f32[5,56,128]{2,1,0:T(8,128)S(1)}, f32[16,48,128]{2,1,0:T(8,128)S(1)}) custom-call(f32[24,56,128]{2,1,0:T(8,128)S(1)} %get-tuple-element.93.extended, f32[56,128]{1,0:T(8,128)S(1)} %get-tuple-element.94.left, f32[56,128]{1,0:T(8,128)S(1)} %get-tuple-element.95.right, ...), custom_call_target="tpu_custom_call" | custom-call | tf_op jit(solution)/shard_map/pallas_call | solution.py:661
  27.2 1.3 %shard_map.101 = f32[480,128]{1,0:T(8,128)S(1)} custom-call(f32[24,56,128]{2,1,0:T(8,128)S(1)} %get-tuple-element.93.extended, f32[56,128]{1,0:T(8,128)S(1)} %get-tuple-element.94.left, f32[56,128]{1,0:T(8,128)S(1)} %get-tuple-element.95.right, f32[56,128]{1,0:T(8,128)S(1)} %get-tuple-element.86.col_first, f32[56,128]{1,0:T(8,128)S(1)} %get-tuple-element.85.col_last, ...), custom_call_target="tpu_custom_call" | custom-call | tf_op jit(solution)/shard_map/pallas_call | solution.py:656
  28.6 2.0 %collective-permute-done.4 = f32[144,128]{1,0:T(8,128)S(1)} collective-permute-done((f32[144,128]{1,0:T(8,128)S(1)}, f32[144,128]{1,0:T(8,128)S(1)}, u32[]{:S(2)}, u32[]{:S(2)}) %collective-permute-start.4) | collective-permute-done | bytes 73760 | tf_op jit(solution)/shard_map/ppermute | solution.py:503
  30.6 0.0 copy-start.2
  30.6 0.0 copy-start.4
  30.6 0.0 copy-start.5
  30.6 0.1 collective-permute-start.5
  30.7 0.6 copy-done.2
  31.3 0.0 copy-done.4
  31.3 0.0 copy-done.5
  31.3 0.7 %shard_map.103 = (f32[2,48,48]{2,1,0:T(8,128)S(1)}, f32[48,128]{1,0:T(8,128)S(1)}, f32[1,1280]{1,0:T(1,128)S(1)}, f32[48,1280]{1,0:T(8,128)S(1)}) custom-call(f32[24,128]{1,0:T(8,128)S(1)} %slice_add_fusion.7.early, s32[1,1280]{1,0:T(1,128)S(1)} %copy-done.5, s32[1,1280]{1,0:T(1,128)S(1)} %copy-done.4, f32[1,1280]{1,0:T(1,128)S(1)} %copy-done.2), custom_call_target="tpu_custom_call" | custom-call | tf_op jit(solution)/shard_map/pallas_call | solution.py:674
  32.0 0.1 collective-permute-done.5
  32.2 1.3 %collective-permute-start.6 = (f32[240,128]{1,0:T(8,128)S(1)}, f32[240,128]{1,0:T(8,128)S(1)}, u32[]{:S(2)}, u32[]{:S(2)}) collective-permute-start(f32[240,128]{1,0:T(8,128)S(1)} %pad_maximum_fusion.4), channel_id=1, source_target_pairs={{0,24},{8,16},{16,8},{24,0},{1,25},{9,17},{17,9},{25,1},{2,26},{10... | collective-permute-start | bytes 368648 | tf_op jit(solution)/shard_map/ppermute | solution.py:503
  33.5 4.1 %shard_map.104 = (f32[48,48]{1,0:T(8,128)S(1)}, f32[48,48]{1,0:T(8,128)S(1)}) custom-call(f32[2,48,48]{2,1,0:T(8,128)S(1)} %get-tuple-element.104.both), custom_call_target="tpu_custom_call" | custom-call | tf_op jit(solution)/shard_map/pallas_call | solution.py:684
  37.7 0.4 collective-permute-start.8
  38.1 0.1 shard_map.105.pieces
  38.2 0.5 collective-permute-start.7
  38.7 3.8 %collective-permute-done.7 = f32[120,128]{1,0:T(8,128)S(1)} collective-permute-done((f32[120,128]{1,0:T(8,128)S(1)}, f32[120,128]{1,0:T(8,128)S(1)}, u32[]{:S(2)}, u32[]{:S(2)}) %collective-permute-start.7) | collective-permute-done | bytes 61472 | tf_op jit(solution)/shard_map/ppermute | solution.py:503
  42.6 0.9 %collective-permute-start.9 = (f32[120,128]{1,0:T(8,128)S(1)}, f32[120,128]{1,0:T(8,128)S(1)}, u32[]{:S(2)}, u32[]{:S(2)}) collective-permute-start(f32[120,128]{1,0:T(8,128)S(1)} %add.113), channel_id=1, source_target_pairs={{0,4},{1,5},{2,6},{3,7},{4,0},{5,1},{6,2},{7,3},{8,12},{9,13},{10,... | collective-permute-start | bytes 184328 | tf_op jit(solution)/shard_map/ppermute | solution.py:503
  43.5 0.3 shard_map.106.weights
  43.9 2.7 %shard_map.107.refs_0_ = f32[8,48,128]{2,1,0:T(8,128)S(1)} custom-call(bf16[96,1280]{1,0:T(8,128)(2,1)S(1)} %shard_map.106.weights, f32[24,56,128]{2,1,0:T(8,128)S(1)} %get-tuple-element.93.extended, f32[20,56,128]{2,1,0:T(8,128)S(1)} %get-tuple-element.117.grad_x, f32[20,56,128]{2,1,0:T(8,128)S(1)} %get-tuple-element.118.grad_y), custom_call_target="tpu_custom_call" | custom-call | flops 3000000000 | bytes 1048576 | tf_op jit(solution)/shard_map/pallas_call | solution.py:703
  46.5 1.3 %collective-permute-done.9 = f32[120,128]{1,0:T(8,128)S(1)} collective-permute-done((f32[120,128]{1,0:T(8,128)S(1)}, f32[120,128]{1,0:T(8,128)S(1)}, u32[]{:S(2)}, u32[]{:S(2)}) %collective-permute-start.9) | collective-permute-done | bytes 61472 | tf_op jit(solution)/shard_map/ppermute | solution.py:503
  47.9 1.9 %collective-permute-start.10 = (f32[120,128]{1,0:T(8,128)S(1)}, f32[120,128]{1,0:T(8,128)S(1)}, u32[]{:S(2)}, u32[]{:S(2)}) collective-permute-start(f32[120,128]{1,0:T(8,128)S(1)} %add.114), channel_id=1, source_target_pairs={{0,2},{1,3},{2,0},{3,1},{4,6},{5,7},{6,4},{7,5},{8,10},{9,11},{10,... | collective-permute-start | bytes 184328 | tf_op jit(solution)/shard_map/ppermute | solution.py:503
  49.7 2.7 %shard_map.108.refs_1_ = f32[8,48,128]{2,1,0:T(8,128)S(1)} custom-call(bf16[96,1280]{1,0:T(8,128)(2,1)S(1)} %shard_map.106.weights, f32[24,56,128]{2,1,0:T(8,128)S(1)} %get-tuple-element.93.extended, f32[20,56,128]{2,1,0:T(8,128)S(1)} %get-tuple-element.117.grad_x, f32[20,56,128]{2,1,0:T(8,128)S(1)} %get-tuple-element.118.grad_y), custom_call_target="tpu_custom_call" | custom-call | flops 3000000000 | bytes 1048576 | tf_op jit(solution)/shard_map/pallas_call | solution.py:703
  52.4 0.4 collective-permute-start.11
  52.8 2.2 %shard_map.109.base = f32[16,48,128]{2,1,0:T(8,128)S(1)} custom-call(bf16[96,1280]{1,0:T(8,128)(2,1)S(1)} %shard_map.106.weights, f32[24,56,128]{2,1,0:T(8,128)S(1)} %get-tuple-element.93.extended, f32[2,56,128]{2,1,0:T(8,128)S(1)} %bitcast.17, f32[2,56,128]{2,1,0:T(8,128)S(1)} %bitcast.16, f32[20,56,128]{2,1,0:T(8,128)S(1)} %get-tuple-element.118.grad_y, ...), custom_call_target="tpu_custom_call" | custom-call | tf_op jit(solution)/shard_map/pallas_call | solution.py:727
  55.0 1.3 %collective-permute-done.11 = f32[120,128]{1,0:T(8,128)S(1)} collective-permute-done((f32[120,128]{1,0:T(8,128)S(1)}, f32[120,128]{1,0:T(8,128)S(1)}, u32[]{:S(2)}, u32[]{:S(2)}) %collective-permute-start.11) | collective-permute-done | bytes 61472 | tf_op jit(solution)/shard_map/ppermute | solution.py:503
  56.3 0.6 collective-permute-start.12
  56.9 1.0 %collective-permute-done.12 = f32[240,128]{1,0:T(8,128)S(1)} collective-permute-done((f32[240,128]{1,0:T(8,128)S(1)}, f32[240,128]{1,0:T(8,128)S(1)}, u32[]{:S(2)}, u32[]{:S(2)}) %collective-permute-start.12) | collective-permute-done | bytes 122912 | tf_op jit(solution)/shard_map/ppermute | solution.py:503
  57.9 1.7 %shard_map.110 = (f32[768,128]{1,0:T(8,128)}, f32[48,128]{1,0:T(8,128)}) custom-call(f32[480,128]{1,0:T(8,128)S(1)} %pad_maximum_fusion.1.tensor, bf16[96,1280]{1,0:T(8,128)(2,1)S(1)} %shard_map.106.weights, bf16[2560,128]{1,0:T(8,128)(2,1)S(1)} %shard_map.105.pieces, f32[48,48]{1,0:T(8,128)S(1)} %get-tuple-element.130.gram_inverse, ...), custom_call_target="tpu_custom_call" | custom-call | tf_op jit(solution)/shard_map/pallas_call | solution.py:735
  (54 shorter events, 0.6 us)
Async XLA Ops:
  0.6 0.7 %copy-start.1 = (s32[128,48]{0,1:T(8,128)S(1)}, s32[128,48]{0,1:T(8,128)}, u32[]{:S(2)}) copy-start(s32[128,48]{0,1:T(8,128)} %param.10) | copy-start | bytes 73732
  0.7 0.7 %copy-start.3 = (f32[2,8,128]{2,1,0:T(8,128)S(1)}, f32[2,8,128]{2,1,0:T(8,128)}, u32[]{:S(2)}) copy-start(f32[2,8,128]{2,1,0:T(8,128)} %param.9) | copy-start | bytes 24580
  0.7 0.7 %copy-start.6 = (s32[8,128]{1,0:T(8,128)S(1)}, s32[8,128]{1,0:T(8,128)}, u32[]{:S(2)}) copy-start(s32[8,128]{1,0:T(8,128)} %water.1) | copy-start | bytes 12292
  0.7 0.7 %copy-start.7 = (f32[48]{0:T(128)S(1)}, f32[48]{0:T(128)}, u32[]{:S(2)}) copy-start(f32[48]{0:T(128)} %param.11) | copy-start | bytes 580
  1.4 1.0 %copy-start = (f32[48,2,8,128]{3,2,1,0:T(8,128)S(1)}, f32[48,2,8,128]{3,2,1,0:T(8,128)}, u32[]{:S(2)}) copy-start(f32[48,2,8,128]{3,2,1,0:T(8,128)} %param.8) | copy-start | bytes 1179652
  3.7 1.7 %collective-permute-start = (f32[600,128]{1,0:T(8,128)S(1)}, f32[600,128]{1,0:T(8,128)S(1)}, u32[]{:S(2)}, u32[]{:S(2)}) collective-permute-start(f32[600,128]{1,0:T(8,128)S(1)} %constant_dynamic-update-slice_fusion), channel_id=1, source_target_pairs={{0,8},{8,0},{16,24},{24,16},{1,9},{9,1},{17,25},{25,17},{2,10},{10... | collective-permute-start | bytes 921608 | tf_op jit(solution)/shard_map/ppermute | solution.py:503
  5.5 6.3 %collective-permute-start.1 = (f32[256,128]{1,0:T(8,128)S(1)}, f32[256,128]{1,0:T(8,128)S(1)}, u32[]{:S(2)}, u32[]{:S(2)}) collective-permute-start(f32[256,128]{1,0:T(8,128)S(1)} %pad_maximum_fusion.3), channel_id=1, source_target_pairs={{0,24},{8,16},{16,8},{24,0},{1,25},{9,17},{17,9},{25,1},{2,26},{10... | collective-permute-start | bytes 393224 | tf_op jit(solution)/shard_map/ppermute | solution.py:503
  12.1 5.4 %collective-permute-start.2 = (f32[200,128]{1,0:T(8,128)S(1)}, f32[200,128]{1,0:T(8,128)S(1)}, u32[]{:S(2)}, u32[]{:S(2)}) collective-permute-start(f32[200,128]{1,0:T(8,128)S(1)} %pad_maximum_fusion.7), channel_id=1, source_target_pairs={{0,1},{1,0},{2,3},{3,2},{4,5},{5,4},{6,7},{7,6},{8,9},{9,8},{10,11... | collective-permute-start | bytes 307208 | tf_op jit(solution)/shard_map/ppermute | solution.py:503
  17.5 7.5 %collective-permute-start.3 = (f32[200,128]{1,0:T(8,128)S(1)}, f32[200,128]{1,0:T(8,128)S(1)}, u32[]{:S(2)}, u32[]{:S(2)}) collective-permute-start(f32[200,128]{1,0:T(8,128)S(1)} %pad_maximum_fusion.8), channel_id=1, source_target_pairs={{0,7},{1,2},{2,1},{3,4},{4,3},{5,6},{6,5},{7,0},{8,15},{9,10},{10,... | collective-permute-start | bytes 307208 | tf_op jit(solution)/shard_map/ppermute | solution.py:503
  25.0 5.5 %collective-permute-start.4 = (f32[144,128]{1,0:T(8,128)S(1)}, f32[144,128]{1,0:T(8,128)S(1)}, u32[]{:S(2)}, u32[]{:S(2)}) collective-permute-start(f32[144,128]{1,0:T(8,128)S(1)} %pad_maximum_fusion.9), channel_id=1, source_target_pairs={{0,4},{1,5},{2,6},{3,7},{4,0},{5,1},{6,2},{7,3},{8,12},{9,13},{10,... | collective-permute-start | bytes 221192 | tf_op jit(solution)/shard_map/ppermute | solution.py:503
  30.6 0.7 %copy-start.2 = (f32[1,1280]{1,0:T(1,128)S(1)}, f32[1,1280]{1,0:T(1,128)}, u32[]{:S(2)}) copy-start(f32[1,1280]{1,0:T(1,128)} %constant.73.clone.share) | copy-start | bytes 15364
  30.6 0.7 %copy-start.4 = (s32[1,1280]{1,0:T(1,128)S(1)}, s32[1,1280]{1,0:T(1,128)}, u32[]{:S(2)}) copy-start(s32[1,1280]{1,0:T(1,128)} %constant.72.clone.second) | copy-start | bytes 15364
  30.6 0.7 %copy-start.5 = (s32[1,1280]{1,0:T(1,128)S(1)}, s32[1,1280]{1,0:T(1,128)}, u32[]{:S(2)}) copy-start(s32[1,1280]{1,0:T(1,128)} %constant.71.clone.first) | copy-start | bytes 15364
  30.6 1.5 %collective-permute-start.5 = (f32[352,128]{1,0:T(8,128)S(1)}, f32[352,128]{1,0:T(8,128)S(1)}, u32[]{:S(2)}, u32[]{:S(2)}) collective-permute-start(f32[352,128]{1,0:T(8,128)S(1)} %pad_maximum_fusion.2), channel_id=1, source_target_pairs={{0,8},{8,0},{16,24},{24,16},{1,9},{9,1},{17,25},{25,17},{2,10},{10... | collective-permute-start | bytes 540680 | tf_op jit(solution)/shard_map/ppermute | solution.py:503
  32.2 5.4 %collective-permute-start.6 = (f32[240,128]{1,0:T(8,128)S(1)}, f32[240,128]{1,0:T(8,128)S(1)}, u32[]{:S(2)}, u32[]{:S(2)}) collective-permute-start(f32[240,128]{1,0:T(8,128)S(1)} %pad_maximum_fusion.4), channel_id=1, source_target_pairs={{0,24},{8,16},{16,8},{24,0},{1,25},{9,17},{17,9},{25,1},{2,26},{10... | collective-permute-start | bytes 368648 | tf_op jit(solution)/shard_map/ppermute | solution.py:503
  37.7 4.9 %collective-permute-start.8 = (f32[240,128]{1,0:T(8,128)S(1)}, f32[240,128]{1,0:T(8,128)S(1)}, u32[]{:S(2)}, u32[]{:S(2)}) collective-permute-start(f32[240,128]{1,0:T(8,128)S(1)} %pad_maximum_fusion.5), channel_id=1, source_target_pairs={{0,8},{8,0},{16,24},{24,16},{1,9},{9,1},{17,25},{25,17},{2,10},{10... | collective-permute-start | bytes 368648 | tf_op jit(solution)/shard_map/ppermute | solution.py:503
  38.2 4.3 %collective-permute-start.7 = (f32[120,128]{1,0:T(8,128)S(1)}, f32[120,128]{1,0:T(8,128)S(1)}, u32[]{:S(2)}, u32[]{:S(2)}) collective-permute-start(f32[120,128]{1,0:T(8,128)S(1)} %get-tuple-element.111), channel_id=1, source_target_pairs={{0,1},{1,0},{2,3},{3,2},{4,5},{5,4},{6,7},{7,6},{8,9},{9,8},{10,11... | collective-permute-start | bytes 184328 | tf_op jit(solution)/shard_map/ppermute | solution.py:503
  42.6 5.3 %collective-permute-start.9 = (f32[120,128]{1,0:T(8,128)S(1)}, f32[120,128]{1,0:T(8,128)S(1)}, u32[]{:S(2)}, u32[]{:S(2)}) collective-permute-start(f32[120,128]{1,0:T(8,128)S(1)} %add.113), channel_id=1, source_target_pairs={{0,4},{1,5},{2,6},{3,7},{4,0},{5,1},{6,2},{7,3},{8,12},{9,13},{10,... | collective-permute-start | bytes 184328 | tf_op jit(solution)/shard_map/ppermute | solution.py:503
  47.9 4.5 %collective-permute-start.10 = (f32[120,128]{1,0:T(8,128)S(1)}, f32[120,128]{1,0:T(8,128)S(1)}, u32[]{:S(2)}, u32[]{:S(2)}) collective-permute-start(f32[120,128]{1,0:T(8,128)S(1)} %add.114), channel_id=1, source_target_pairs={{0,2},{1,3},{2,0},{3,1},{4,6},{5,7},{6,4},{7,5},{8,10},{9,11},{10,... | collective-permute-start | bytes 184328 | tf_op jit(solution)/shard_map/ppermute | solution.py:503
  52.4 3.9 %collective-permute-start.11 = (f32[120,128]{1,0:T(8,128)S(1)}, f32[120,128]{1,0:T(8,128)S(1)}, u32[]{:S(2)}, u32[]{:S(2)}) collective-permute-start(f32[120,128]{1,0:T(8,128)S(1)} %add.115), channel_id=1, source_target_pairs={{0,24},{8,16},{16,8},{24,0},{1,25},{9,17},{17,9},{25,1},{2,26},{10... | collective-permute-start | bytes 184328 | tf_op jit(solution)/shard_map/ppermute | solution.py:503
  56.3 1.5 %collective-permute-start.12 = (f32[240,128]{1,0:T(8,128)S(1)}, f32[240,128]{1,0:T(8,128)S(1)}, u32[]{:S(2)}, u32[]{:S(2)}) collective-permute-start(f32[240,128]{1,0:T(8,128)S(1)} %pad_maximum_fusion.6), channel_id=1, source_target_pairs={{0,8},{8,0},{16,24},{24,16},{1,9},{9,1},{17,25},{25,17},{2,10},{10... | collective-permute-start | bytes 368648 | tf_op jit(solution)/shard_map/ppermute | solution.py:503
